TPU v7x, 32 devices: a whole 2x2x4 slice. The times are simulated.
32 devices in a mesh: rep: 4 (over x, core), tile: 8 (over z, y).
Axes of the slice: x: 2, y: 2, z: 4, core: 2. Of those that a mesh axis runs over, the one named last changes fastest.
Arguments:
- fields: bfloat16 [4, 192, 8, 8, 256], P('rep', 'tile'), may hold values from -6 to 6
- cotangent: bfloat16 [4, 192, 8, 8, 256], P('rep', 'tile'), may hold values from -6 to 6
- weights: float32 [4, 2304, 256], P('rep', 'tile'), may hold values from -6 to 6
- ema: float32 [4, 2304, 256], P('rep', 'tile'), may hold values from -6 to 6
- tile_links: int32 [192, 4], replicated, may hold values from 0 to 191, as said below
- tile_codes: int32 [192, 4], replicated, may hold values from 0 to 3
- corner_links: int32 [192, 4], replicated, may hold values from -1 to 191, as said below
- corner_codes: int32 [192, 4], replicated, may hold values from 0 to 3
- gossip_bit: int32 [1], replicated, may hold values from 0 to 1
- batch_size: int32 [1], replicated, may hold values from 32 to 512
Outputs:
- activations: bfloat16 [4, 192, 8, 8, 256], P('rep', 'tile')
- field_grad: bfloat16 [4, 192, 8, 8, 256], P('rep', 'tile')
- averaged: float32 [4, 2304, 256], P('rep', 'tile')
- ema_out: float32 [4, 2304, 256], P('rep', 'tile')
Inputs may be any that keep to these rules, and one draw needn't show every extreme that they name: tile_links, tile_codes, corner_links and corner_codes describe the tiles of a HEALPix sphere: 12 base faces, each cut into 4 x 4 tiles, numbered face by face (the order of the faces drawn from the seed) and row by row within a face. The relation is symmetric: if tile u lies across edge q of tile t as its edge e, then t lies across edge e of u as its edge q, and cells along a shared edge run in the same order on both tiles; likewise, if corner q of t takes corner cell c of u, then corner c of u takes corner cell q of t. `corner_links`: -1 exactly at the tiles' corners that touch one of the 8 vertices where only three base faces meet.
All inputs are finite; a program needn't handle non-finite values.
Results may differ from a plain program's by a relative error of at most 0.0014.
The roundings to bfloat16 on the way count: a program that leaves them out, or rounds other values in their place, can miss the bound.
Values may be sent and summed in bfloat16 or wider, within the bound.
A program may use at most 64 MiB of HBM per device.

v0:
```python
import jax
import jax.numpy as jnp
from jax import lax
from jax.sharding import PartitionSpec as P

LEARN = 0.5


def from_partner(value, axis, distance):
    mask = 2**distance
    pairs = [(source, source ^ mask) for source in range(lax.axis_size(axis))]
    return lax.ppermute(value, axis, pairs)


def swap_level(level):

    def run_swap(value):
        return from_partner(value, "rep", level)

    return run_swap


def edge_strips(block):
    return jnp.stack([block[:, 0], block[:, -1], block[:, :, 0], block[:, :, -1]], axis=1)


def corner_cells(block):
    return jnp.stack([block[:, 0, 0], block[:, 0, -1], block[:, -1, 0], block[:, -1, -1]], axis=1)


def padded_sides(block):
    return jnp.stack(
        [block[:, 0, 1:-1], block[:, -1, 1:-1], block[:, 1:-1, 0], block[:, 1:-1, -1]], axis=1
    )


def body(
    fields,
    cotangent,
    weights,
    ema,
    tile_links,
    tile_codes,
    corner_links,
    corner_codes,
    gossip_bit,
    batch_size,
):
    block = fields[0]
    per_device = block.shape[0]
    side_len = block.shape[1]
    channels = block.shape[-1]
    first_tile = lax.axis_index("tile") * per_device
    my_tiles = first_tile + jnp.arange(per_device, dtype=jnp.int32)
    my_links = lax.dynamic_slice_in_dim(tile_links, first_tile, per_device, 0)
    my_codes = lax.dynamic_slice_in_dim(tile_codes, first_tile, per_device, 0)
    my_corner = lax.dynamic_slice_in_dim(corner_links, first_tile, per_device, 0)
    my_corner_codes = lax.dynamic_slice_in_dim(corner_codes, first_tile, per_device, 0)
    my_present = (my_corner >= 0)[:, :, None]
    quarter = jnp.arange(4, dtype=jnp.int32)
    strips_in = lax.all_gather(edge_strips(block), "tile", axis=0, tiled=True)
    cells_in = lax.all_gather(corner_cells(block), "tile", axis=0, tiled=True)
    row_count = strips_in.shape[0]
    source = jnp.arange(row_count, dtype=jnp.int32)
    choose = (
        (my_links[:, :, None, None] == source[None, None, :, None])
        & (my_codes[:, :, None, None] == quarter[None, None, None, :])
    ).astype(jnp.bfloat16)
    gained = jnp.einsum(
        "tepq,pqsc->tesc", choose, strips_in, preferred_element_type=jnp.float32
    ).astype(jnp.bfloat16)
    corner_pick = (
        (my_corner[:, :, None, None] == source[None, None, :, None])
        & (my_corner_codes[:, :, None, None] == quarter[None, None, None, :])
    ).astype(jnp.bfloat16)
    gained_cells = jnp.einsum(
        "tkpq,pqc->tkc", corner_pick, cells_in, preferred_element_type=jnp.float32
    ).astype(jnp.bfloat16)
    top_row = jnp.concatenate([gained_cells[:, 0:1], gained[:, 0], gained_cells[:, 1:2]], axis=1)
    bottom_row = jnp.concatenate([gained_cells[:, 2:3], gained[:, 1], gained_cells[:, 3:4]], axis=1)
    middle = jnp.concatenate([gained[:, 2][:, :, None], block, gained[:, 3][:, :, None]], axis=2)
    padded = jnp.concatenate([top_row[:, None], middle, bottom_row[:, None]], axis=1)
    weight_scale = (9.0 * channels) ** (-0.5)
    w_local = weights[0]
    w_scaled = (w_local * weight_scale).astype(jnp.bfloat16)
    gathered = lax.all_gather(w_scaled, "tile", axis=0, tiled=True)
    kernel = gathered.reshape(channels, 9, channels)
    hidden = jnp.zeros((per_device * side_len * side_len, channels), jnp.float32)
    for tap_index in range(9):
        row_off, col_off = divmod(tap_index, 3)
        window = padded[:, row_off : row_off + side_len, col_off : col_off + side_len].reshape(
            -1, channels
        )
        hidden = hidden + jnp.dot(
            window, kernel[:, tap_index, :], preferred_element_type=jnp.float32
        )
    sigmoid_pre = jax.nn.sigmoid(hidden)
    output = (hidden * sigmoid_pre).astype(jnp.bfloat16)
    grad_pre = (
        cotangent[0].reshape(-1, channels).astype(jnp.float32)
        * (sigmoid_pre * (1.0 + hidden * (1.0 - sigmoid_pre)))
    ).astype(jnp.bfloat16)
    grad_pad = jnp.zeros((per_device, side_len + 2, side_len + 2, channels), jnp.float32)
    for tap_index in range(9):
        row_off, col_off = divmod(tap_index, 3)
        backward = jnp.dot(grad_pre, kernel[:, tap_index, :].T, preferred_element_type=jnp.float32)
        grad_pad = grad_pad.at[:, row_off : row_off + side_len, col_off : col_off + side_len].add(
            backward.reshape(per_device, side_len, side_len, channels)
        )
    row_count = w_local.shape[0] * lax.axis_size("tile")
    chan_count = row_count // 9
    pieces = []
    for tap_index in range(9):
        row_off, col_off = divmod(tap_index, 3)
        window = padded[:, row_off : row_off + side_len, col_off : col_off + side_len].reshape(
            -1, chan_count
        )
        pieces.append(jnp.dot(window.T, grad_pre, preferred_element_type=jnp.float32))
    kernel_grad = lax.psum_scatter(
        jnp.stack(pieces, axis=1).reshape(row_count, channels),
        "tile",
        scatter_dimension=0,
        tiled=True,
    )
    side_grads = padded_sides(grad_pad).astype(jnp.bfloat16)
    corner_grads = jnp.where(my_present, corner_cells(grad_pad), jnp.zeros((), jnp.float32)).astype(
        jnp.bfloat16
    )
    sides_in = lax.all_gather(side_grads, "tile", axis=0, tiled=True)
    corners_in = lax.all_gather(corner_grads, "tile", axis=0, tiled=True)
    route = (
        (tile_links[:, :, None, None] == my_tiles[None, None, :, None])
        & (tile_codes[:, :, None, None] == quarter[None, None, None, :])
    ).astype(jnp.bfloat16)
    added = jnp.einsum("petq,pesc->tqsc", route, sides_in, preferred_element_type=jnp.float32)
    corner_route = (
        (corner_links[:, :, None, None] == my_tiles[None, None, :, None])
        & (corner_codes[:, :, None, None] == quarter[None, None, None, :])
    ).astype(jnp.bfloat16)
    corner_added = jnp.einsum(
        "pktq,pkc->tqc", corner_route, corners_in, preferred_element_type=jnp.float32
    )
    interior = grad_pad[:, 1:-1, 1:-1]
    interior = interior.at[:, 0].add(added[:, 0]).at[:, -1].add(added[:, 1])
    interior = interior.at[:, :, 0].add(added[:, 2]).at[:, :, -1].add(added[:, 3])
    interior = interior.at[:, 0, 0].add(corner_added[:, 0]).at[:, 0, -1].add(corner_added[:, 1])
    interior = interior.at[:, -1, 0].add(corner_added[:, 2]).at[:, -1, -1].add(corner_added[:, 3])
    square_sum = lax.psum(jnp.sum(kernel_grad * kernel_grad), "tile")
    root_mean = jnp.sqrt(square_sum / (9.0 * channels * channels) + 1e-06)
    updated = w_local - LEARN * kernel_grad / root_mean
    level_count = lax.axis_size("rep").bit_length() - 1
    branches = [swap_level(level) for level in range(level_count)]
    partner_rows = lax.switch(jnp.clip(gossip_bit[0], 0, level_count - 1), branches, updated)
    averaged = 0.5 * (updated + partner_rows)
    decay = jnp.power(0.99, batch_size[0].astype(jnp.float32) / 32.0)
    ema_out = decay * ema[0] + (1.0 - decay) * averaged
    return (
        output.reshape(1, per_device, side_len, side_len, channels),
        interior.astype(jnp.bfloat16)[None],
        averaged[None],
        ema_out[None],
    )


def solution(mesh):
    return jax.shard_map(
        body,
        mesh=mesh,
        in_specs=(
            P("rep", "tile", None, None, None),
            P("rep", "tile", None, None, None),
            P("rep", "tile", None),
            P("rep", "tile", None),
            P(),
            P(),
            P(),
            P(),
            P(),
            P(),
        ),
        out_specs=(
            P("rep", "tile", None, None, None),
            P("rep", "tile", None, None, None),
            P("rep", "tile", None),
            P("rep", "tile", None),
        ),
        check_vma=False,
    )
```

profile of v0, /device:TPU:0, one launch (start us, length us, event | category | flops | bytes accessed | tf_op | source)
XLA Modules:
  0.0 325.5 jit_solution(11753589489019267710)
XLA Ops:
  7.2 1.6 fusion.40
  8.9 1.6 copy.326
  10.6 1.3 slice.795
  11.9 0.8 pad_maximum_fusion.3
  13.1 33.6 %all_gather.15 = bf16[192,4,256]{2,0,1:T(8,128)(2,1)S(1)} all-gather(bf16[24,4,256]{2,0,1:T(8,128)(2,1)S(1)} %pad_maximum_fusion.5), channel_id=1, replica_groups=mesh['rep'=4,'tile'=8] {'tile'}, dimensions={0}, use_global_device_ids=true | all-gather | bytes 442368 | tf_op jit(solution)/shard_map/all_gather | solution.py:62
  47.2 8.4 %all-gather.6.cloned.1.call-done = bf16[2304,256]{1,0:T(8,128)(2,1)} async-done(((bf16[288,256]{1,0:T(8,128)(2,1)}), bf16[2304,256]{1,0:T(8,128)(2,1)}) %all-gather.6.cloned.1.call-update) | async-done | bytes 1179664 | tf_op jit(solution)/shard_map/all_gather | solution.py:86
  55.6 2.3 reshape.801
  58.0 2.7 fusion.90
  61.7 55.8 %all-gather.4.cloned.1.call-done = bf16[192,4,8,256]{3,0,2,1:T(8,128)(2,1)} async-done(((bf16[24,4,8,256]{3,0,2,1:T(8,128)(2,1)}), bf16[192,4,8,256]{3,0,2,1:T(8,128)(2,1)}) %all-gather.4.cloned.1.call-update) | async-done | bytes 3145744 | tf_op jit(solution)/shard_map/all_gather | solution.py:61
  117.5 2.7 fusion.16
  128.2 1.9 fusion.9
  134.1 3.5 %copy.164 = f32[256,9,256]{2,1,0:T(8,128)} copy(f32[256,9,256]{2,0,1:T(8,128)S(1)} %fusion.19) | data formatting | bytes 4718592 | tf_op jit(solution)/shard_map/stack | solution.py:120
  137.6 4.5 %reshape.822 = f32[2304,256]{1,0:T(8,128)} reshape(f32[256,9,256]{2,1,0:T(8,128)} %copy.164) | data formatting | bytes 4718592 | tf_op jit(solution)/shard_map/reshape | solution.py:120
  143.6 0.8 and_reduce_fusion
  144.8 2.4 scatter-add.56
  147.2 1.7 dynamic-slice_add_fusion
  148.9 10.8 %scatter-add.59 = f32[24,10,10,256]{3,2,1,0:T(8,128)} dynamic-update-slice(f32[24,10,10,256]{3,2,1,0:T(8,128)} %scatter-add.56, f32[24,8,8,256]{3,2,1,0:T(8,128)S(1)} %dynamic-slice_add_fusion, s32[]{:T(128)} %constant.499.clone.1, s32[]{:T(128)} %bitcast.49, s32[]{:T(128)} %bitcast.50, s32[]{:T(128)} %constant.499.clone.1) | dynamic-update-slice | bytes 3145732 | tf_op jit(solution)/shard_map/scatter-add | solution.py:107
  159.7 4.3 %add_select_fusion = f32[24,8,8,256]{3,2,1,0:T(8,128)S(1)} fusion(f32[24,10,10,256]{3,2,1,0:T(8,128)} %scatter-add.59, s32[]{:T(128)} %bitcast.53, s32[]{:T(128)} %bitcast.54, bf16[24,8,8,256]{3,2,1,0:T(8,128)(2,1)S(1)} %bitcast.319, pred[]{:T(512)} %get-tuple-element.276, bf16[256,1,256]{2,1,0:T(2,128)(2,1)S(1)} %copy-done.9), kind=kOutput, calls=%fused_computation.15 | convolution fusion | flops 202113024 | bytes 4063241 | tf_op jit(solution)/shard_map/dot_general | solution.py:106
  164.0 10.7 %scatter-add.60 = f32[24,10,10,256]{3,2,1,0:T(8,128)} dynamic-update-slice(f32[24,10,10,256]{3,2,1,0:T(8,128)} %scatter-add.59, f32[24,8,8,256]{3,2,1,0:T(8,128)S(1)} %add_select_fusion, s32[]{:T(128)} %constant.499.clone.1, s32[]{:T(128)} %bitcast.53, s32[]{:T(128)} %bitcast.54, s32[]{:T(128)} %constant.499.clone.1) | dynamic-update-slice | bytes 3145732 | tf_op jit(solution)/shard_map/scatter-add | solution.py:107
  174.7 3.2 fusion.8
  177.9 2.3 slice_add_fusion.3
  180.2 9.5 %scatter-add.64 = f32[24,10,10,256]{3,2,1,0:T(8,128)} dynamic-update-slice(f32[24,10,10,256]{3,2,1,0:T(8,128)} %fusion.8, f32[24,8,8,256]{3,2,1,0:T(8,128)S(1)} %slice_add_fusion.3, s32[]{:T(128)} %constant.499.clone.1, s32[]{:T(128)} %constant.508.clone.1, s32[]{:T(128)} %constant.508.clone.1, s32[]{:T(128)} %constant.499.clone.1) | dynamic-update-slice | bytes 3145732 | tf_op jit(solution)/shard_map/scatter-add | solution.py:107
  189.7 2.3 slice_add_fusion.2
  192.0 9.5 %scatter-add.65 = f32[24,10,10,256]{3,2,1,0:T(8,128)} dynamic-update-slice(f32[24,10,10,256]{3,2,1,0:T(8,128)} %scatter-add.64, f32[24,8,8,256]{3,2,1,0:T(8,128)S(1)} %slice_add_fusion.2, s32[]{:T(128)} %constant.499.clone.1, s32[]{:T(128)} %constant.508.clone.1, s32[]{:T(128)} %constant.505.clone.1, s32[]{:T(128)} %constant.499.clone.1) | dynamic-update-slice | bytes 3145732 | tf_op jit(solution)/shard_map/scatter-add | solution.py:107
  201.5 3.1 fusion.7
  204.6 2.3 slice_add_fusion
  206.9 9.4 %scatter-add.69 = f32[24,10,10,256]{3,2,1,0:T(8,128)} dynamic-update-slice(f32[24,10,10,256]{3,2,1,0:T(8,128)} %fusion.7, f32[24,8,8,256]{3,2,1,0:T(8,128)S(1)} %slice_add_fusion, s32[]{:T(128)} %constant.499.clone.1, s32[]{:T(128)} %constant.505.clone.1, s32[]{:T(128)} %constant.508.clone.1, s32[]{:T(128)} %constant.499.clone.1) | dynamic-update-slice | bytes 3145732 | tf_op jit(solution)/shard_map/scatter-add | solution.py:107
  216.4 2.1 slice.824
  219.3 1.8 copy.148
  221.1 10.0 %scatter-add.70 = f32[24,10,10,256]{3,2,1,0:T(8,128)} dynamic-update-slice(f32[24,10,10,256]{3,2,1,0:T(8,128)} %scatter-add.69, f32[24,8,8,256]{3,2,1,0:T(8,128)} %copy.148, s32[]{:T(128)} %constant.499.clone.1, s32[]{:T(128)} %constant.505.clone.1, s32[]{:T(128)} %constant.505.clone.1, s32[]{:T(128)} %constant.499.clone.1) | dynamic-update-slice | bytes 3145732 | tf_op jit(solution)/shard_map/scatter-add | solution.py:107
  231.0 2.4 convert.13
  233.9 0.8 pad_maximum_fusion.4
  237.0 1.2 slice_bitcast_fusion.8
  238.3 32.1 %all_gather.19 = bf16[192,4,256]{2,1,0:T(4,128)(2,1)S(1)} all-gather(bf16[24,4,256]{2,1,0:T(4,128)(2,1)S(1)} %fusion.71), channel_id=1, replica_groups=mesh['rep'=4,'tile'=8] {'tile'}, dimensions={0}, use_global_device_ids=true | all-gather | bytes 442368 | tf_op jit(solution)/shard_map/all_gather | solution.py:130
  270.7 1.6 multiply_reduce_fusion
  272.3 2.3 slice.825
  274.6 19.6 %psum.7 = f32[]{:T(128)} all-reduce(f32[]{:T(128)} %multiply_reduce_fusion), channel_id=1, replica_groups=mesh['rep'=4,'tile'=8] {'tile'}, use_global_device_ids=true, to_apply=%region_4.0 | all-reduce | flops 1 | bytes 8 | tf_op jit(solution)/shard_map/psum | solution.py:148
  294.9 6.9 %conditional.1 = (f32[288,256]{1,0:T(8,128)}) conditional(s32[]{:T(128)} %bitcast.102, f32[288,256]{1,0:T(8,128)S(1)} %bitcast_subtract_fusion, f32[288,256]{1,0:T(8,128)S(1)} %bitcast_subtract_fusion), branch_computations={%region_5.0_spmd, %region_6.0_spmd} | conditional | bytes 1179696 | solution.py:153
  294.9 1.5 collective-permute-start.1
  296.5 5.4 %collective-permute-done.1 = f32[288,256]{1,0:T(8,128)} collective-permute-done((f32[288,256]{1,0:T(8,128)S(1)}, f32[288,256]{1,0:T(8,128)}, u32[]{:S(2)}, u32[]{:S(2)}) %collective-permute-start.1) | collective-permute-done | bytes 294944 | tf_op jit(solution)/shard_map/cond/branch_1_fun/ppermute | solution.py:12
  301.8 1.8 fusion.39
  303.7 3.9 %fusion.13 = f32[24,4,8,256]{3,0,2,1:T(8,128)S(1)} fusion(bf16[192,4,8,256]{3,2,1,0:T(8,128)(2,1)} %all-gather.8.cloned.1.call-done, pred[192,4,4]{0,1,2:T(4,128)(4,1)S(1)} %iota_compare_fusion.3, pred[192,4,24]{0,2,1:T(8,128)(4,1)S(1)} %get-tuple-element.270), kind=kOutput, calls=%fused_computation.30 | convolution fusion | flops 302063616 | bytes 3953664 | tf_op jit(solution)/shard_map/petq,pesc->tqsc/dot_general | solution.py:135
  307.6 1.1 fusion.42
  309.0 2.4 scatter-add.75
  311.7 2.4 scatter-add.76
  314.3 1.9 broadcast_select_fusion
  316.2 1.4 scatter-add.80
  318.0 1.0 convert_bitcast_fusion
  (136 shorter events, 19.5 us)
Async XLA Ops:
  7.2 48.5 %all-gather.6.cloned.1.call-start = ((), (), s32[]{:S(2)}) async-start(), calls=%async_computation.2 | async-start | bytes 1327104 | tf_op jit(solution)/shard_map/all_gather | solution.py:86
  8.9 108.6 %all-gather.4.cloned.1.call-start = ((), (), s32[]{:S(2)}) async-start(), calls=%async_computation.1 | async-start | bytes 3538944 | tf_op jit(solution)/shard_map/all_gather | solution.py:61
  10.5 2.3 copy-start.20
  10.5 2.4 copy-start.18
  10.5 2.4 copy-start.17
  10.5 2.4 copy-start.19
  12.8 257.9 %reduce-scatter.2.cloned.1.call-start = ((), (), s32[]{:S(2)}) async-start(), calls=%async_computation.4 | async-start | bytes 2654208 | tf_op jit(solution)/shard_map/reduce_scatter | solution.py:119
  58.0 3.4 %copy-start = (bf16[1,24,8,8,256]{4,3,2,1,0:T(8,128)(2,1)S(1)}, bf16[1,24,8,8,256]{4,3,2,1,0:T(8,128)(2,1)}, u32[]{:S(2)}) copy-start(bf16[1,24,8,8,256]{4,3,2,1,0:T(8,128)(2,1)} %param.46) | copy-start | bytes 2359300
  60.6 0.7 copy-start.5
  122.0 1.0 copy-start.12
  122.4 1.0 copy-start.10
  123.3 0.9 copy-start.8
  124.3 0.9 copy-start.7
  125.2 0.9 copy-start.4
  127.0 1.0 copy-start.14
  127.0 1.2 copy-start.23
  130.9 1.1 copy-start.1
  142.1 1.5 copy-start.21
  142.1 1.5 copy-start.22
  142.1 2.2 copy-start.13
  142.1 161.6 %all-gather.8.cloned.1.call-start = ((), (), s32[]{:S(2)}) async-start(), calls=%async_computation.3 | async-start | bytes 3538944 | tf_op jit(solution)/shard_map/all_gather | solution.py:129
  144.7 2.4 copy-start.11
  148.9 10.8 %copy-start.9 = (bf16[256,1,256]{2,1,0:T(2,128)(2,1)S(1)}, bf16[256,1,256]{2,1,0:T(2,128)(2,1)}, u32[]{:S(2)}) copy-start(bf16[256,1,256]{2,1,0:T(2,128)(2,1)} %get-tuple-element.224) | copy-start | bytes 393220
  174.7 3.2 copy-start.6
  216.4 2.1 copy-start.15
  272.3 22.6 %copy-start.2 = (f32[1,288,256]{2,1,0:T(8,128)S(1)}, f32[1,288,256]{2,1,0:T(8,128)}, u32[]{:S(2)}) copy-start(f32[1,288,256]{2,1,0:T(8,128)} %param.48) | copy-start | bytes 884740
  272.3 22.6 %copy-start.3 = (f32[288,256]{1,0:T(8,128)S(1)}, f32[288,256]{1,0:T(8,128)}, u32[]{:S(2)}) copy-start(f32[288,256]{1,0:T(8,128)} %reduce-scatter.2.cloned.1.call-done) | copy-start | bytes 884740
  272.3 29.5 %copy-start.16 = (f32[1,288,256]{2,1,0:T(8,128)S(1)}, f32[1,288,256]{2,1,0:T(8,128)}, u32[]{:S(2)}) copy-start(f32[1,288,256]{2,1,0:T(8,128)} %param.49) | copy-start | bytes 884740
  294.9 6.9 %collective-permute-start.1 = (f32[288,256]{1,0:T(8,128)S(1)}, f32[288,256]{1,0:T(8,128)}, u32[]{:S(2)}, u32[]{:S(2)}) collective-permute-start(f32[288,256]{1,0:T(8,128)S(1)} %param.35), channel_id=1, source_target_pairs={{0,16},{8,24},{16,0},{24,8},{1,17},{9,25},{17,1},{25,9},{2,18},{10... | collective-permute-start | bytes 884744 | tf_op jit(solution)/shard_map/cond/branch_1_fun/ppermute | solution.py:12
Sparse Core Ops, SparseCore 0:
  10.8 44.8 all-gather.5
  58.4 59.0 all-gather.3
  142.2 67.4 reduce-scatter.1
  234.8 61.4 all-gather.7
where the time goes:
time: 325 us; the launch traced here: 326 us
  local copies, waits for them, and re-layouts  101 us (31%)
  blocking collectives  85.3 us (26%)
  waiting for transfers between devices  69.6 us (21%)
  matrix products  36 us (11%)
  between operations  16.6 us (5%)
  other arithmetic  15.6 us (5%)
    scatter-add x7, local copies, waits for them, and re-layouts, body(): grad_pad.at[:, row_off:row_off + side_len, col_off:col_off + side_len]  62.3 us
    all_gather x1, waiting for transfers between devices, body(): strips_in = lax.all_gather(edge_strips(block), 'tile', axis=0, tiled=True)  55.8 us
    all_gather x1, blocking collectives, body(): cells_in = lax.all_gather(corner_cells(block), 'tile', axis=0, tiled=True)  33.6 us
    all_gather x1, blocking collectives, body(): corners_in = lax.all_gather(corner_grads, 'tile', axis=0, tiled=True)  32.1 us
    dot_general x9, matrix products, body(): jnp.dot(grad_pre, kernel[:, tap_index, :].T, preferred_element_type=jnp.f...  20.3 us
    psum x1, blocking collectives, body(): square_sum = lax.psum(jnp.sum(kernel_grad * kernel_grad), 'tile')  19.6 us
    all_gather x1, waiting for transfers between devices, body(): gathered = lax.all_gather(w_scaled, 'tile', axis=0, tiled=True)  8.39 us
  transfers between devices with their start and end apart: 5, of which 3 were waited for; matrix products, arithmetic and copies ran while one was open for 34% of the time, Pallas kernels for 0%

commit v1 on v0

v1 whole, which is shorter than its diff:
```python
import functools
import math

import jax
import jax.numpy as jnp
import numpy as np
from jax import lax
from jax.experimental import pallas as pl
from jax.experimental.pallas import tpu as pltpu
from jax.sharding import PartitionSpec as P

LEARN = 0.5
MESH = pl.DeviceIdType.MESH
VMEM = pl.BlockSpec(memory_space=pltpu.VMEM)
SMEM = pl.BlockSpec(memory_space=pltpu.SMEM)
LIMIT = 48 * 1024 * 1024
LANES = 128


def strip_lists(tiles, devices):
    sub = math.isqrt(tiles // 12)
    per = tiles // devices
    lists = [[] for _ in range(devices)]
    slot = np.full((tiles, 4), -1, np.int32)
    for tile in range(tiles):
        face, row, col = tile // (sub * sub), tile % (sub * sub) // sub, tile % sub
        owner = tile // per
        for edge, (down, right) in enumerate(((-1, 0), (1, 0), (0, -1), (0, 1))):
            r, c = row + down, col + right
            inside = 0 <= r < sub and 0 <= c < sub
            if inside and (face * sub * sub + r * sub + c) // per == owner:
                continue
            slot[tile, edge] = len(lists[owner])
            lists[owner].append((tile - owner * per) * 4 + edge)
    most = max(len(found) for found in lists)
    table = np.zeros((devices, most), np.int32)
    for owner, found in enumerate(lists):
        table[owner, : len(found)] = found
    return most, table, np.maximum(slot, 0)


def greet(peers):
    barrier = pltpu.get_barrier_semaphore()
    for peer in peers:
        pl.semaphore_signal(barrier, inc=1, device_id=peer, device_id_type=MESH)
    pl.semaphore_wait(barrier, len(peers))


def tile_peers(n):
    me = lax.axis_index("tile")
    return [{"tile": lax.rem(me + k, n)} for k in range(1, n)]


def send(src, dst, send_sem, recv_sem, peer):
    copy = pltpu.make_async_remote_copy(
        src_ref=src,
        dst_ref=dst,
        send_sem=send_sem,
        recv_sem=recv_sem,
        device_id=peer,
        device_id_type=MESH,
    )
    copy.start()
    return copy


def pack_strips(index, strips, corners, pack, count):
    @pl.loop(0, count)
    def _(k):
        pack[k] = strips[index[k]]

    pack[count:] = corners[...]


def gather_kernel(n, count, index, taps, strips, corners, all_taps, all_pack, pack, s1, r1, s2, r2):
    me = lax.axis_index("tile")
    peers = tile_peers(n)
    greet(peers)
    copies = []
    for k, peer in enumerate(peers):
        copies.append(send(taps, all_taps.at[me], s1.at[k], r1.at[k], peer))
    pack_strips(index, strips, corners, pack, count)
    for k, peer in enumerate(peers):
        copies.append(send(pack, all_pack.at[me], s2.at[k], r2.at[k], peer))
    all_taps[me] = taps[...]
    for copy in copies:
        copy.wait()


def put(ref, rows, value):
    for half in range(ref.shape[0]):
        ref[half, rows] = value[:, half * LANES : (half + 1) * LANES]


def get(ref, rows):
    return jnp.concatenate([ref[half, rows] for half in range(ref.shape[0])], axis=1)


def gain(ref, rows, value):
    for half in range(ref.shape[0]):
        ref[half, rows] = ref[half, rows] + value[:, half * LANES : (half + 1) * LANES]


def find_strip(refs, strips, all_pack, t, edge):
    me_ref, links, codes, _, _, slots = refs
    per = strips.shape[0] // 4
    at = t * 4 + edge
    link, code = links[at], codes[at]
    me = me_ref[0]
    owner = link // per
    here = jnp.clip((link - me * per) * 4 + code, 0, per * 4 - 1)
    own = strips[here].astype(jnp.float32)
    other = all_pack[owner, slots[link * 4 + code]].astype(jnp.float32)
    return jnp.where(owner == me, own, other)


def find_corner(refs, corners, all_pack, count, t, q):
    me_ref, _, _, corner_links, corner_codes, _ = refs
    per = corners.shape[0] * 2
    at = t * 4 + q
    link, code = corner_links[at], corner_codes[at]
    me = me_ref[0]
    safe = jnp.maximum(link, 0)
    owner = safe // per
    near = safe - owner * per
    own = corners[near // 2].astype(jnp.float32)
    other = all_pack[owner, count + near // 2].astype(jnp.float32)
    rows = jnp.where(owner == me, own, other)
    row = lax.rem(near, 2) * 4 + code
    chosen = lax.broadcasted_iota(jnp.int32, rows.shape, 0) == row
    chosen = chosen & (link >= 0)
    return jnp.sum(jnp.where(chosen, rows, 0.0), axis=0, keepdims=True)


def main_kernel(
    n, count, me_ref, links, codes, corner_links, corner_codes, slots,
    fields, cot, all_taps, all_pack, strips, corners,
    act, wgrad, inner, side_out, corner_out,
    e0, e1, e2, x0, x1, x2, kern, dpre, d0, d1, d2,
):
    refs = (me_ref, links, codes, corner_links, corner_codes, slots)
    side, wide = fields.shape[0], fields.shape[1]
    per = wide // side
    rc = all_taps.shape[2]
    f32 = jnp.float32
    for owner in range(n):
        for tap in range(9):
            kern[tap, owner * rc : (owner + 1) * rc] = all_taps[owner, tap]
    for i in range(side):
        put(e1, pl.ds((i + 1) * wide, wide), fields[i].astype(f32))

    @pl.loop(0, per)
    def _(t):
        at = pl.multiple_of(t * side, side)
        put(e1, pl.ds(at, side), find_strip(refs, strips, all_pack, t, 0))
        put(e1, pl.ds((side + 1) * wide + at, side), find_strip(refs, strips, all_pack, t, 1))

    for i in range(side + 2):
        rows = pl.ds(i * wide, wide)
        for half in range(e1.shape[0]):
            e0[half, rows] = pltpu.roll(e1[half, rows], 1, 0)
            e2[half, rows] = pltpu.roll(e1[half, rows], wide - 1, 0)

    @pl.loop(0, per)
    def _(t):
        at = t * side
        end = (side + 1) * wide + at
        put(e0, pl.ds(wide + at, side, stride=wide), find_strip(refs, strips, all_pack, t, 2))
        put(e2, pl.ds(wide + at + side - 1, side, stride=wide), find_strip(refs, strips, all_pack, t, 3))
        put(e0, pl.ds(at, 1), find_corner(refs, corners, all_pack, count, t, 0))
        put(e2, pl.ds(at + side - 1, 1), find_corner(refs, corners, all_pack, count, t, 1))
        put(e0, pl.ds(end, 1), find_corner(refs, corners, all_pack, count, t, 2))
        put(e2, pl.ds(end + side - 1, 1), find_corner(refs, corners, all_pack, count, t, 3))

    for x, e in ((x0, e0), (x1, e1), (x2, e2)):
        for half in range(e.shape[0]):
            x[:, half * LANES : (half + 1) * LANES] = e[half].astype(jnp.bfloat16)
    xs = (x0, x1, x2)

    dpre[0 : 2 * wide] = jnp.zeros((2 * wide, dpre.shape[1]), jnp.bfloat16)
    dpre[(side + 2) * wide :] = jnp.zeros((2 * wide, dpre.shape[1]), jnp.bfloat16)

    @pl.loop(0, side)
    def _(i):
        pre = None
        for tap in range(9):
            a, b = divmod(tap, 3)
            rows = xs[b][pl.ds(pl.multiple_of((i + a) * wide, 16), wide)]
            part = jnp.dot(rows, kern[tap], preferred_element_type=f32)
            pre = part if pre is None else pre + part
        s = jax.nn.sigmoid(pre)
        act[i] = (pre * s).astype(jnp.bfloat16)
        grad = cot[i].astype(f32) * (s * (1.0 + pre * (1.0 - s)))
        dpre[pl.ds(pl.multiple_of((i + 2) * wide, 16), wide)] = grad.astype(jnp.bfloat16)

    for tap in range(9):
        a, b = divmod(tap, 3)
        part = lax.dot_general(
            xs[b][a * wide : (a + side) * wide],
            dpre[2 * wide : (side + 2) * wide],
            (((0,), (0,)), ((), ())),
            preferred_element_type=f32,
        )
        for owner in range(n):
            wgrad[owner, tap] = part[owner * rc : (owner + 1) * rc].astype(jnp.bfloat16)

    @pl.loop(0, side + 2)
    def _(i):
        at = pl.multiple_of(i * wide, 16)
        found = []
        for b, d in enumerate((d0, d1, d2)):
            total = None
            for a in range(3):
                rows = dpre[pl.ds(pl.multiple_of((i - a + 2) * wide, 16), wide)]
                part = lax.dot_general(
                    rows, kern[3 * a + b], (((1,), (1,)), ((), ())), preferred_element_type=f32
                )
                total = part if total is None else total + part
            found.append(total)
        put(d0, pl.ds(at, wide), found[0])
        put(d2, pl.ds(at, wide), found[2])
        column = lax.rem(lax.broadcasted_iota(jnp.int32, found[0].shape, 0), side)
        left = jnp.where(column < side - 1, pltpu.roll(found[0], wide - 1, 0), 0.0)
        right = jnp.where(column > 0, pltpu.roll(found[2], 1, 0), 0.0)
        put(d1, pl.ds(at, wide), found[1] + left + right)

    inner[...] = d1[:, wide : (side + 1) * wide]
    last = (side + 1) * wide

    @pl.loop(0, per)
    def _(t):
        at = pl.multiple_of(t * side, side)
        side_out[t * 4] = get(d1, pl.ds(at, side)).astype(jnp.bfloat16)
        side_out[t * 4 + 1] = get(d1, pl.ds(last + at, side)).astype(jnp.bfloat16)
        side_out[t * 4 + 2] = get(d0, pl.ds(wide + at, side, stride=wide)).astype(jnp.bfloat16)
        side_out[t * 4 + 3] = get(d2, pl.ds(wide + at + side - 1, side, stride=wide)).astype(jnp.bfloat16)

    for pair in range(per // 2):
        rows = []
        for t in (2 * pair, 2 * pair + 1):
            at = t * side
            for d, row in ((d0, at), (d2, at + side - 1), (d0, last + at), (d2, last + at + side - 1)):
                rows.append(get(d, pl.ds(row, 1)))
        corner_out[pair] = jnp.concatenate(rows, axis=0).astype(jnp.bfloat16)


def reduce_kernel(
    n, count, levels, total_count, index, bit, wgrad, strips, corners, weights,
    averaged, all_pack,
    pack, slots, sums, updated, partner, s1, r1, s2, r2, s3, r3, s4, r4,
):
    me = lax.axis_index("tile")
    rep = lax.axis_index("rep")
    peers = tile_peers(n)
    friends = []
    for level in range(levels):
        step = 2**level
        friends.append({"rep": rep + step * (1 - 2 * lax.rem(rep // step, 2))})
    greet(peers + friends)
    copies = []
    for k, peer in enumerate(peers):
        copies.append(
            send(wgrad.at[lax.rem(me + k + 1, n)], slots.at[k], s1.at[k], r1.at[k], peer)
        )
    pack_strips(index, strips, corners, pack, count)
    packs = []
    for k, peer in enumerate(peers):
        packs.append(send(pack, all_pack.at[me], s2.at[k], r2.at[k], peer))
    grad = wgrad[me].astype(jnp.float32)
    for k, copy in enumerate(copies):
        copy.wait()
        grad = grad + slots[k].astype(jnp.float32)
    square = grad * grad
    lanes = sums.shape[2]
    square = jnp.sum(square.reshape(-1, 8, square.shape[2]), axis=0)
    sums[0] = sum(square[:, j : j + lanes] for j in range(0, square.shape[1], lanes))
    small = []
    for k, peer in enumerate(peers):
        small.append(send(sums.at[0], sums.at[k + 1], s3.at[k], r3.at[k], peer))
    for copy in small:
        copy.wait()
    mean = jnp.sum(sums[...], keepdims=True) / total_count
    updated[...] = weights[...] - LEARN * grad / jnp.sqrt(mean + 1e-06)
    swaps = []
    for level, friend in enumerate(friends):
        swaps.append(send(updated, partner.at[level], s4.at[level], r4.at[level], friend))
    for copy in swaps:
        copy.wait()
    averaged[...] = 0.5 * (updated[...] + partner[bit[0]])
    for copy in packs:
        copy.wait()


def finish_kernel(
    count, me_ref, links, codes, corner_links, corner_codes, slots,
    inner, all_pack, strips, corners, out, total,
):
    refs = (me_ref, links, codes, corner_links, corner_codes, slots)
    side, wide = out.shape[0], out.shape[1]
    per = wide // side
    total[...] = inner[...]
    last = (side - 1) * wide

    @pl.loop(0, per)
    def _(t):
        at = pl.multiple_of(t * side, side)
        first = pl.ds(at, side)
        gain(total, first, find_strip(refs, strips, all_pack, t, 0))
        end = pl.ds(last + at, side)
        gain(total, end, find_strip(refs, strips, all_pack, t, 1))
        left = pl.ds(at, side, stride=wide)
        gain(total, left, find_strip(refs, strips, all_pack, t, 2))
        right = pl.ds(at + side - 1, side, stride=wide)
        gain(total, right, find_strip(refs, strips, all_pack, t, 3))
        for q, row in enumerate((at, at + side - 1, last + at, last + at + side - 1)):
            cell = pl.ds(row, 1)
            gain(total, cell, find_corner(refs, corners, all_pack, count, t, q))

    for i in range(side):
        out[i] = get(total, pl.ds(i * wide, wide)).astype(jnp.bfloat16)


def body(
    fields, cotangent, weights, ema, tile_links, tile_codes, corner_links, corner_codes,
    gossip_bit, batch_size,
):
    block = fields[0]
    per, side, _, channels = block.shape
    n = lax.axis_size("tile")
    levels = lax.axis_size("rep").bit_length() - 1
    me = lax.axis_index("tile")
    count, table, slot_table = strip_lists(tile_links.shape[0], n)
    rows = weights.shape[1]
    rc = rows // 9
    bf16, f32 = jnp.bfloat16, jnp.float32
    total_count = 9.0 * channels * channels
    index = lax.dynamic_slice_in_dim(jnp.asarray(table), me, 1, 0)[0]
    blocks = count + per // 2

    def mine(array):
        return lax.dynamic_slice_in_dim(array, me * per, per, 0).reshape(-1)

    tables = (
        me.astype(jnp.int32).reshape(1),
        mine(tile_links),
        mine(tile_codes),
        mine(corner_links),
        mine(corner_codes),
        jnp.asarray(slot_table.reshape(-1)),
    )
    w_tap = weights[0].reshape(rc, 9, channels).transpose(1, 0, 2)
    taps = (w_tap * total_count_scale(channels)).astype(bf16)
    strips = jnp.stack([block[:, 0], block[:, -1], block[:, :, 0], block[:, :, -1]], axis=1)
    strips = strips.reshape(per * 4, side, channels)
    cells = jnp.stack(
        [block[:, 0, 0], block[:, 0, -1], block[:, -1, 0], block[:, -1, -1]], axis=1
    ).reshape(per // 2, 8, channels)

    params = functools.partial(pltpu.CompilerParams, vmem_limit_bytes=LIMIT)
    sems = [pltpu.SemaphoreType.DMA((n - 1,))] * 2
    pack_shape = pltpu.VMEM((blocks, side, channels), bf16)
    all_pack_shape = jax.ShapeDtypeStruct((n, blocks, side, channels), bf16)
    all_taps, all_pack = pl.pallas_call(
        functools.partial(gather_kernel, n, count),
        out_shape=(jax.ShapeDtypeStruct((n, 9, rc, channels), bf16), all_pack_shape),
        in_specs=[SMEM, VMEM, VMEM, VMEM],
        out_specs=(VMEM, VMEM),
        scratch_shapes=[pack_shape] + sems * 2,
        compiler_params=params(collective_id=0, has_side_effects=True),
    )(index, taps, strips, cells)

    wide = per * side

    def by_row(value):
        return value.transpose(1, 0, 2, 3).reshape(side, wide, channels)

    def by_tile(value):
        return value.reshape(side, per, side, channels).transpose(1, 0, 2, 3)[None]

    tall = (side + 2) * wide
    act, wgrad, inner, side_grads, corner_grads = pl.pallas_call(
        functools.partial(main_kernel, n, count),
        out_shape=(
            jax.ShapeDtypeStruct((side, wide, channels), bf16),
            jax.ShapeDtypeStruct((n, 9, rc, channels), bf16),
            jax.ShapeDtypeStruct((channels // LANES, side * wide, LANES), f32),
            jax.ShapeDtypeStruct((per * 4, side, channels), bf16),
            jax.ShapeDtypeStruct((per // 2, 8, channels), bf16),
        ),
        in_specs=[SMEM] * 6 + [VMEM] * 6,
        out_specs=(VMEM,) * 5,
        scratch_shapes=[pltpu.VMEM((channels // LANES, tall, LANES), f32)] * 3
        + [pltpu.VMEM((tall, channels), bf16)] * 3
        + [pltpu.VMEM((9, channels, channels), bf16)]
        + [pltpu.VMEM(((side + 4) * wide, channels), bf16)]
        + [pltpu.VMEM((channels // LANES, tall, LANES), f32)] * 3,
        compiler_params=params(),
    )(*tables, by_row(block), by_row(cotangent[0]), all_taps, all_pack, strips, cells)

    bit = jnp.clip(gossip_bit, 0, levels - 1)
    averaged, all_back = pl.pallas_call(
        functools.partial(reduce_kernel, n, count, levels, total_count),
        out_shape=(jax.ShapeDtypeStruct((9, rc, channels), f32), all_pack_shape),
        in_specs=[SMEM, SMEM, VMEM, VMEM, VMEM, VMEM],
        out_specs=(VMEM, VMEM),
        scratch_shapes=[
            pack_shape,
            pltpu.VMEM((n - 1, 9, rc, channels), bf16),
            pltpu.VMEM((n, 8, 128), f32),
            pltpu.VMEM((9, rc, channels), f32),
            pltpu.VMEM((levels, 9, rc, channels), f32),
        ]
        + sems * 3
        + [pltpu.SemaphoreType.DMA((levels,))] * 2,
        compiler_params=params(collective_id=1, has_side_effects=True),
    )(index, bit, wgrad, side_grads, corner_grads, w_tap)

    grads = pl.pallas_call(
        functools.partial(finish_kernel, count),
        out_shape=jax.ShapeDtypeStruct((side, wide, channels), bf16),
        in_specs=[SMEM] * 6 + [VMEM] * 4,
        out_specs=VMEM,
        scratch_shapes=[pltpu.VMEM((channels // LANES, side * wide, LANES), f32)],
        compiler_params=params(),
    )(*tables, inner, all_back, side_grads, corner_grads)

    averaged = averaged.transpose(1, 0, 2).reshape(rows, channels)
    decay = jnp.power(0.99, batch_size[0].astype(f32) / 32.0)
    ema_out = decay * ema[0] + (1.0 - decay) * averaged
    return by_tile(act), by_tile(grads), averaged[None], ema_out[None]


def total_count_scale(channels):
    return (9.0 * channels) ** (-0.5)


def solution(mesh):
    wide = P("rep", "tile", None, None, None)
    thin = P("rep", "tile", None)
    return jax.shard_map(
        body,
        mesh=mesh,
        in_specs=(wide, wide, thin, thin, P(), P(), P(), P(), P(), P()),
        out_specs=(wide, wide, thin, thin),
        check_vma=False,
    )
```

time: 325 us -> 160 us (0.49)
  Pallas kernels: 0 us -> 149 us
  local copies, waits for them, and re-layouts: 101 us -> 7.61 us
  blocking collectives: 85.3 us -> 0 us
  waiting for transfers between devices: 69.6 us -> 0 us
  matrix products: 36 us -> 0 us
  other arithmetic: 15.6 us -> 1.01 us
  between operations: 16.6 us -> 2.4 us
    pallas_call x0 -> x4, Pallas kernels: none -> 149 us  [the longest x1 76.5 us: body(): pl.pallas_call(functools.partial(reduce_kernel, n, count, levels, total_c...]
    scatter-add x13 -> x0, local copies, waits for them, and re-layouts: 68.9 us -> none  [the longest x7 62.3 us: body(): grad_pad.at[:, row_off:row_off + side_len, col_off:col_off + side_len]]
    all_gather x2 -> x0, blocking collectives: 65.7 us -> none  [the longest x1 33.6 us: body(): cells_in = lax.all_gather(corner_cells(block), 'tile', axis=0, tiled=True)]
    all_gather x3 -> x0, waiting for transfers between devices: 64.2 us -> none  [the longest x1 55.8 us: body(): strips_in = lax.all_gather(edge_strips(block), 'tile', axis=0, tiled=True)]
    dot_general x31 -> x0, matrix products: 36 us -> none  [the longest x9 20.3 us: body(): jnp.dot(grad_pre, kernel[:, tap_index, :].T, preferred_element_type=jnp.f...]
    psum x1 -> x0, blocking collectives: 19.6 us -> none  [body(): square_sum = lax.psum(jnp.sum(kernel_grad * kernel_grad), 'tile')]
    another operation x10 -> x5, local copies, waits for them, and re-layouts: 8.58 us -> 0.17 us  [the longest x1 0.05 us: body(): return (by_tile(act), by_tile(grads), averaged[None], ema_out[None])]
    slice x19 -> x4, local copies, waits for them, and re-layouts: 8.33 us -> 0.45 us  [the longest x2 0.32 us: body(): block[:, 0]]
  transfers between devices with their start and end apart: 5 -> 0, of which waited for: 3 -> 0; matrix products, arithmetic and copies ran while one was open for 34% -> 0% of each run, Pallas kernels for 0% -> 0%
where the time goes in v1:
time: 160 us
  Pallas kernels  149 us (93%)
  local copies, waits for them, and re-layouts  7.61 us (5%)
  between operations  2.4 us (2%)
    pallas_call x1, Pallas kernels, body(): pl.pallas_call(functools.partial(reduce_kernel, n, count, levels, total_c...  76.5 us
    pallas_call x1, Pallas kernels, body(): pl.pallas_call(functools.partial(gather_kernel, n, count), out_shape=(jax...  50.9 us
    pallas_call x1, Pallas kernels, body(): pl.pallas_call(functools.partial(main_kernel, n, count), out_shape=(jax.S...  18.3 us
    pallas_call x1, Pallas kernels, body(): pl.pallas_call(functools.partial(finish_kernel, count), out_shape=jax.Sha...  3.47 us

profile of v1, /device:TPU:0, one launch (start us, length us, event | category | flops | bytes accessed | tf_op | source)
XLA Modules:
  0.0 160.2 jit_solution(3318299193672165586)
XLA Ops:
  0.6 0.0 copy-start
  0.6 1.4 copy.111
  2.0 0.1 fusion.1
  2.2 0.3 fusion.2
  2.5 0.0 copy-start.6
  2.5 0.1 copy.88
  2.5 0.1 copy.89
  2.6 0.1 pad_maximum_fusion
  2.7 0.0 copy-start.8
  2.7 0.0 copy-start.9
  2.8 0.0 copy-start.10
  2.8 0.0 copy-start.11
  2.8 0.0 copy-start.4
  2.8 0.8 fusion.index
  3.6 0.0 copy-done.6
  3.6 0.2 multiply_convert_fusion
  3.8 50.9 %shard_map.147 = (bf16[8,9,32,256]{3,2,1,0:T(8,128)(2,1)S(1)}, bf16[8,40,8,256]{3,2,1,0:T(8,128)(2,1)S(1)}) custom-call(s32[28]{0:T(128)S(1)} %fusion.index, bf16[9,32,256]{2,1,0:T(8,128)(2,1)S(1)} %get-tuple-element.22.taps, bf16[96,8,256]{2,1,0:T(8,128)(2,1)S(1)} %bitcast.51, bf16[12,8,256]{2,1,0:T(8,128)(2,1)S(1)} %reshape.65.corners), custom_call_target="tpu_custom_call" | custom-call | tf_op jit(solution)/shard_map/pallas_call | solution.py:363
  54.7 0.0 copy-start.2
  54.7 1.1 copy-done.2
  55.8 0.0 copy-done.8
  55.8 0.1 constant_dynamic-slice_fusion.3
  55.9 0.1 copy.80
  55.9 0.1 reshape.58.links
  56.0 0.1 copy.81
  56.1 0.1 reshape.59.codes
  56.2 0.0 copy-done.10
  56.2 0.0 copy-done.11
  56.3 0.1 constant_dynamic-slice_fusion.1
  56.3 0.1 copy.82
  56.4 0.1 reshape.60.corner_links
  56.5 0.1 copy.83
  56.6 0.1 reshape.61.corner_codes
  56.7 0.0 copy-done
  56.7 0.0 copy-done.4
  56.7 0.0 copy-start.3
  56.7 0.2 copy_bitcast_fusion
  56.9 0.5 copy-done.3
  57.4 18.3 %shard_map.148 = (bf16[8,192,256]{2,1,0:T(8,128)(2,1)S(1)}, bf16[8,9,32,256]{3,2,1,0:T(8,128)(2,1)S(1)}, f32[2,1536,128]{2,1,0:T(8,128)}, bf16[96,8,256]{2,1,0:T(8,128)(2,1)S(1)}, bf16[12,8,256]{2,1,0:T(8,128)(2,1)S(1)}) custom-call(s32[1]{0:T(128)} %bitcast.me_ref, s32[96]{0:T(128)S(1)} %reshape.58.links, s32[96]{0:T(128)S(1)} %reshape.59.codes, ...), custom_call_target="tpu_custom_call" | custom-call | tf_op jit(solution)/shard_map/pallas_call | solution.py:381
  76.5 76.5 %shard_map.149 = (f32[9,32,256]{2,1,0:T(8,128)S(1)}, bf16[8,40,8,256]{3,2,1,0:T(8,128)(2,1)S(1)}) custom-call(s32[28]{0:T(128)S(1)} %fusion.index, s32[1]{0:T(128)S(6)} %min.6.bit, bf16[8,9,32,256]{3,2,1,0:T(8,128)(2,1)S(1)} %get-tuple-element.17.wgrad, bf16[96,8,256]{2,1,0:T(8,128)(2,1)S(1)} %get-tuple-element.18.strips, ...), custom_call_target="tpu_custom_call" | custom-call | tf_op jit(solution)/shard_map/pallas_call | solution.py:401
  153.0 0.0 copy-done.1
  153.0 3.5 %shard_map.150 = bf16[8,192,256]{2,1,0:T(8,128)(2,1)S(1)} custom-call(s32[1]{0:T(128)} %bitcast.me_ref, s32[96]{0:T(128)S(1)} %reshape.58.links, s32[96]{0:T(128)S(1)} %reshape.59.codes, s32[96]{0:T(128)S(1)} %reshape.60.corner_links, s32[96]{0:T(128)S(1)} %reshape.61.corner_codes, s32[768]{0:T(1024)S(1)} %copy-done.3, f32[2,1536,128]{2,1,0:T(8,128)S(1)} %copy-done.1, ...), custom_call_target="tpu_custom_call" | custom-call | tf_op jit(solution)/shard_map/pallas_call | solution.py:418
  156.5 0.0 copy-start.7
  156.5 1.0 copy_bitcast_fusion.1
  157.5 0.2 copy.94
  157.7 0.1 broadcast_in_dim_reshape.3
  157.7 0.0 copy-start.5
  158.4 0.8 multiply_add_fusion
  159.2 1.0 copy_bitcast_fusion.2
  (12 shorter events, 0.2 us)
Async XLA Ops:
  0.6 56.1 %copy-start = (bf16[1,24,8,8,256]{4,3,2,1,0:T(8,128)(2,1)S(1)}, bf16[1,24,8,8,256]{4,3,2,1,0:T(8,128)(2,1)}, u32[]{:S(2)}) copy-start(bf16[1,24,8,8,256]{4,3,2,1,0:T(8,128)(2,1)} %param.13) | copy-start | bytes 2359300
  2.5 1.1 copy-start.6
  2.7 53.1 %copy-start.8 = (s32[192,4]{0,1:T(4,128)S(1)}, s32[192,4]{0,1:T(4,128)}, u32[]{:S(2)}) copy-start(s32[192,4]{0,1:T(4,128)} %param.17) | copy-start | bytes 9220
  2.7 53.0 %copy-start.9 = (s32[192,4]{0,1:T(4,128)S(1)}, s32[192,4]{0,1:T(4,128)}, u32[]{:S(2)}) copy-start(s32[192,4]{0,1:T(4,128)} %param.16) | copy-start | bytes 9220
  2.8 53.5 %copy-start.10 = (s32[192,4]{0,1:T(4,128)S(1)}, s32[192,4]{0,1:T(4,128)}, u32[]{:S(2)}) copy-start(s32[192,4]{0,1:T(4,128)} %param.19) | copy-start | bytes 9220
  2.8 53.5 %copy-start.11 = (s32[192,4]{0,1:T(4,128)S(1)}, s32[192,4]{0,1:T(4,128)}, u32[]{:S(2)}) copy-start(s32[192,4]{0,1:T(4,128)} %param.18) | copy-start | bytes 9220
  2.8 54.0 %copy-start.4 = (bf16[1,24,8,8,256]{4,3,2,1,0:T(8,128)(2,1)S(1)}, bf16[1,24,8,8,256]{4,3,2,1,0:T(8,128)(2,1)}, u32[]{:S(2)}) copy-start(bf16[1,24,8,8,256]{4,3,2,1,0:T(8,128)(2,1)} %param.12) | copy-start | bytes 2359300
  54.7 1.1 copy-start.2
  56.7 0.7 copy-start.3
  75.8 77.2 %copy-start.1 = (f32[2,1536,128]{2,1,0:T(8,128)S(1)}, f32[2,1536,128]{2,1,0:T(8,128)}, u32[]{:S(2)}) copy-start(f32[2,1536,128]{2,1,0:T(8,128)} %get-tuple-element.16.inner) | copy-start | bytes 4718596
  156.5 1.9 %copy-start.7 = (f32[1,288,256]{2,1,0:T(8,128)S(1)}, f32[1,288,256]{2,1,0:T(8,128)}, u32[]{:S(2)}) copy-start(f32[1,288,256]{2,1,0:T(8,128)} %param.15) | copy-start | bytes 884740
  157.7 2.4 %copy-start.5 = (f32[1,288,256]{2,1,0:T(8,128)}, f32[1,288,256]{2,1,0:T(8,128)S(1)}, u32[]{:S(2)}) copy-start(f32[1,288,256]{2,1,0:T(8,128)S(1)} %broadcast_in_dim_reshape.3) | copy-start | bytes 884740

commit v2 on v1

--- a/solution.py
+++ b/solution.py
@@ -72,19 +72,56 @@
     pack[count:] = corners[...]
 
 
+class Gather:
+    def __init__(self, n, src, dst, sends, recvs):
+        self.n, self.dst, self.sends, self.recvs = n, dst, sends, recvs
+        me = lax.axis_index("tile")
+        self.me = me
+        self.mate = {"tile": me + 1 - 2 * lax.rem(me, 2)}
+        self.first = []
+        for k in range(1, n // 2):
+            peer = {"tile": lax.rem(me + 2 * k, n)}
+            self.first.append(send(src, dst.at[me], sends.at[k - 1], recvs.at[k - 1], peer))
+        at = n // 2 - 1
+        self.rest = [send(src, dst.at[me], sends.at[at], recvs.at[at], self.mate)]
+
+    def forward(self):
+        for k, copy in enumerate(self.first):
+            copy.wait_recv()
+            block = self.dst.at[lax.rem(self.me + self.n - 2 * (k + 1), self.n)]
+            at = self.n // 2 + k
+            self.rest.append(send(block, block, self.sends.at[at], self.recvs.at[at], self.mate))
+
+    def finish(self):
+        for copy in self.first:
+            copy.wait_send()
+        for copy in self.rest:
+            copy.wait()
+
+
 def gather_kernel(n, count, index, taps, strips, corners, all_taps, all_pack, pack, s1, r1, s2, r2):
-    me = lax.axis_index("tile")
-    peers = tile_peers(n)
-    greet(peers)
-    copies = []
-    for k, peer in enumerate(peers):
-        copies.append(send(taps, all_taps.at[me], s1.at[k], r1.at[k], peer))
+    greet(tile_peers(n))
+    one = Gather(n, taps, all_taps, s1, r1)
     pack_strips(index, strips, corners, pack, count)
-    for k, peer in enumerate(peers):
-        copies.append(send(pack, all_pack.at[me], s2.at[k], r2.at[k], peer))
-    all_taps[me] = taps[...]
-    for copy in copies:
-        copy.wait()
+    two = Gather(n, pack, all_pack, s2, r2)
+    all_taps[lax.axis_index("tile")] = taps[...]
+    one.forward()
+    two.forward()
+    one.finish()
+    two.finish()
+
+
+STEPS = 32000.0
+
+
+def encode(value, code, scale):
+    top = jnp.maximum(jnp.max(jnp.abs(value), axis=1, keepdims=True), 1e-30)
+    code[...] = jnp.round(value * (STEPS / top)).astype(jnp.int32).astype(jnp.int16)
+    scale[...] = top * (1.0 / STEPS)
+
+
+def decode(code, scale):
+    return code[...].astype(jnp.int32).astype(jnp.float32) * scale[...]
 
 
 def put(ref, rows, value):
@@ -202,7 +239,7 @@
             preferred_element_type=f32,
         )
         for owner in range(n):
-            wgrad[owner, tap] = part[owner * rc : (owner + 1) * rc].astype(jnp.bfloat16)
+            wgrad[owner, tap] = part[owner * rc : (owner + 1) * rc]
 
     @pl.loop(0, side + 2)
     def _(i):
@@ -247,7 +284,8 @@
 def reduce_kernel(
     n, count, levels, total_count, index, bit, wgrad, strips, corners, weights,
     averaged, all_pack,
-    pack, slots, sums, updated, partner, s1, r1, s2, r2, s3, r3, s4, r4,
+    pack, out_y, out_ys, in_y, in_ys, out_z, out_zs, in_z, in_zs, sums, updated, partner,
+    s1, r1, s2, r2, s3, r3, s4, r4, s5, r5, s6, r6, s7, r7,
 ):
     me = lax.axis_index("tile")
     rep = lax.axis_index("rep")
@@ -257,38 +295,56 @@
         step = 2**level
         friends.append({"rep": rep + step * (1 - 2 * lax.rem(rep // step, 2))})
     greet(peers + friends)
-    copies = []
-    for k, peer in enumerate(peers):
-        copies.append(
-            send(wgrad.at[lax.rem(me + k + 1, n)], slots.at[k], s1.at[k], r1.at[k], peer)
+    line = n // 2
+    odd = lax.rem(me, 2)
+    mate = {"tile": me + 1 - 2 * odd}
+    order = list(range(1, line)) + [0]
+    near, far = {}, {}
+    for k in order:
+        there = lax.rem(me - odd + 2 * k, n) + 1 - odd
+        encode(wgrad[there], out_y.at[k], out_ys.at[k])
+        near[k] = (
+            send(out_y.at[k], in_y.at[k], s1.at[k], r1.at[k], mate),
+            send(out_ys.at[k], in_ys.at[k], s2.at[k], r2.at[k], mate),
         )
     pack_strips(index, strips, corners, pack, count)
-    packs = []
-    for k, peer in enumerate(peers):
-        packs.append(send(pack, all_pack.at[me], s2.at[k], r2.at[k], peer))
-    grad = wgrad[me].astype(jnp.float32)
-    for k, copy in enumerate(copies):
-        copy.wait()
-        grad = grad + slots[k].astype(jnp.float32)
+    halo = Gather(n, pack, all_pack, s7, r7)
+    grad = None
+    for k in order:
+        for copy in near[k]:
+            copy.wait()
+        there = lax.rem(me + 2 * k, n)
+        grad = wgrad[there] + decode(in_y.at[k], in_ys.at[k])
+        if k > 0:
+            encode(grad, out_z.at[k - 1], out_zs.at[k - 1])
+            peer = {"tile": there}
+            far[k] = (
+                send(out_z.at[k - 1], in_z.at[k - 1], s3.at[k - 1], r3.at[k - 1], peer),
+                send(out_zs.at[k - 1], in_zs.at[k - 1], s4.at[k - 1], r4.at[k - 1], peer),
+            )
+    halo.forward()
+    for k in far:
+        for copy in far[k]:
+            copy.wait()
+        grad = grad + decode(in_z.at[k - 1], in_zs.at[k - 1])
     square = grad * grad
     lanes = sums.shape[2]
     square = jnp.sum(square.reshape(-1, 8, square.shape[2]), axis=0)
     sums[0] = sum(square[:, j : j + lanes] for j in range(0, square.shape[1], lanes))
     small = []
     for k, peer in enumerate(peers):
-        small.append(send(sums.at[0], sums.at[k + 1], s3.at[k], r3.at[k], peer))
+        small.append(send(sums.at[0], sums.at[k + 1], s5.at[k], r5.at[k], peer))
     for copy in small:
         copy.wait()
     mean = jnp.sum(sums[...], keepdims=True) / total_count
     updated[...] = weights[...] - LEARN * grad / jnp.sqrt(mean + 1e-06)
     swaps = []
     for level, friend in enumerate(friends):
-        swaps.append(send(updated, partner.at[level], s4.at[level], r4.at[level], friend))
+        swaps.append(send(updated, partner.at[level], s6.at[level], r6.at[level], friend))
     for copy in swaps:
         copy.wait()
     averaged[...] = 0.5 * (updated[...] + partner[bit[0]])
-    for copy in packs:
-        copy.wait()
+    halo.finish()
 
 
 def finish_kernel(
@@ -327,6 +383,7 @@
     block = fields[0]
     per, side, _, channels = block.shape
     n = lax.axis_size("tile")
+    line = n // 2
     levels = lax.axis_size("rep").bit_length() - 1
     me = lax.axis_index("tile")
     count, table, slot_table = strip_lists(tile_links.shape[0], n)
@@ -382,7 +439,7 @@
         functools.partial(main_kernel, n, count),
         out_shape=(
             jax.ShapeDtypeStruct((side, wide, channels), bf16),
-            jax.ShapeDtypeStruct((n, 9, rc, channels), bf16),
+            jax.ShapeDtypeStruct((n, 9, rc, channels), f32),
             jax.ShapeDtypeStruct((channels // LANES, side * wide, LANES), f32),
             jax.ShapeDtypeStruct((per * 4, side, channels), bf16),
             jax.ShapeDtypeStruct((per // 2, 8, channels), bf16),
@@ -405,13 +462,23 @@
         out_specs=(VMEM, VMEM),
         scratch_shapes=[
             pack_shape,
-            pltpu.VMEM((n - 1, 9, rc, channels), bf16),
+            pltpu.VMEM((line, 9, rc, channels), jnp.int16),
+            pltpu.VMEM((line, 9, 1, channels), f32),
+            pltpu.VMEM((line, 9, rc, channels), jnp.int16),
+            pltpu.VMEM((line, 9, 1, channels), f32),
+            pltpu.VMEM((line - 1, 9, rc, channels), jnp.int16),
+            pltpu.VMEM((line - 1, 9, 1, channels), f32),
+            pltpu.VMEM((line - 1, 9, rc, channels), jnp.int16),
+            pltpu.VMEM((line - 1, 9, 1, channels), f32),
             pltpu.VMEM((n, 8, 128), f32),
             pltpu.VMEM((9, rc, channels), f32),
             pltpu.VMEM((levels, 9, rc, channels), f32),
         ]
-        + sems * 3
-        + [pltpu.SemaphoreType.DMA((levels,))] * 2,
+        + [pltpu.SemaphoreType.DMA((line,))] * 4
+        + [pltpu.SemaphoreType.DMA((line - 1,))] * 4
+        + sems
+        + [pltpu.SemaphoreType.DMA((levels,))] * 2
+        + sems,
         compiler_params=params(collective_id=1, has_side_effects=True),
     )(index, bit, wgrad, side_grads, corner_grads, w_tap)
 

time: 160 us -> 122 us (0.76)
  Pallas kernels: 149 us -> 107 us
  local copies, waits for them, and re-layouts: 7.61 us -> 10.9 us
    pallas_call x1, Pallas kernels: 76.5 us -> 46 us  [body(): pl.pallas_call(functools.partial(reduce_kernel, n, count, levels, total_c...]
    pallas_call x1, Pallas kernels: 50.9 us -> 39.5 us  [body(): pl.pallas_call(functools.partial(gather_kernel, n, count), out_shape=(jax...]
    unnamed x27 -> x33, local copies, waits for them, and re-layouts: 3.03 us -> 5.13 us
where the time goes in v2:
time: 122 us; the launch traced here: 121 us
  Pallas kernels  107 us (88%)
  local copies, waits for them, and re-layouts  10.9 us (9%)
  between operations  2.28 us (2%)
    pallas_call x1, Pallas kernels, body(): pl.pallas_call(functools.partial(reduce_kernel, n, count, levels, total_c...  46 us
    pallas_call x1, Pallas kernels, body(): pl.pallas_call(functools.partial(gather_kernel, n, count), out_shape=(jax...  39.5 us
    pallas_call x1, Pallas kernels, body(): pl.pallas_call(functools.partial(main_kernel, n, count), out_shape=(jax.S...  18.4 us
    unnamed x33, local copies, waits for them, and re-layouts  5.13 us
    pallas_call x1, Pallas kernels, body(): pl.pallas_call(functools.partial(finish_kernel, count), out_shape=jax.Sha...  3.47 us

profile of v2, /device:TPU:0, one launch (start us, length us, event | category | flops | bytes accessed | tf_op | source)
XLA Modules:
  0.0 121.4 jit_solution(13844554319591824012)
XLA Ops:
  0.6 0.0 copy-start
  0.6 1.4 %copy.111 = bf16[1,24,8,8,256]{4,2,1,3,0:T(8,128)(2,1)S(1)} copy(bf16[1,24,8,8,256]{4,3,2,1,0:T(8,128)(2,1)} %param.12) | data formatting | bytes 1572864 | tf_op args[0]
  2.0 0.1 fusion.1
  2.2 0.3 fusion.2
  2.5 0.0 copy-start.9
  2.5 0.1 copy.88
  2.5 0.1 copy.89
  2.6 0.1 pad_maximum_fusion
  2.7 0.0 copy-start.11
  2.7 0.0 copy-start.12
  2.7 0.0 copy-start.13
  2.8 0.0 copy-start.14
  2.8 0.7 fusion.index
  3.5 0.0 copy-done.9
  3.5 0.2 multiply_convert_fusion
  3.7 39.5 %shard_map.147 = (bf16[8,9,32,256]{3,2,1,0:T(8,128)(2,1)S(1)}, bf16[8,40,8,256]{3,2,1,0:T(8,128)(2,1)S(1)}) custom-call(s32[28]{0:T(128)S(1)} %fusion.index, bf16[9,32,256]{2,1,0:T(8,128)(2,1)S(1)} %get-tuple-element.22.taps, bf16[96,8,256]{2,1,0:T(8,128)(2,1)S(1)} %bitcast.51, bf16[12,8,256]{2,1,0:T(8,128)(2,1)S(1)} %reshape.65.corners), custom_call_target="tpu_custom_call" | custom-call | tf_op jit(solution)/shard_map/pallas_call | solution.py:420
  43.2 0.0 copy-start.3
  43.2 1.0 copy-done.3
  44.3 0.0 copy-done.11
  44.3 0.0 copy-done.12
  44.3 0.1 constant_dynamic-slice_fusion.3
  44.3 0.1 copy.80
  44.4 0.1 reshape.58.links
  44.5 0.1 copy.81
  44.6 0.1 reshape.59.codes
  44.7 0.0 copy-done.13
  44.7 0.1 constant_dynamic-slice_fusion.1
  44.8 0.1 copy.82
  44.9 0.1 reshape.60.corner_links
  45.0 0.1 copy.83
  45.1 0.1 reshape.61.corner_codes
  45.2 0.0 copy-start.7
  45.2 1.4 %copy_bitcast_fusion = (bf16[8,192,256]{2,1,0:T(8,128)(2,1)S(1)}, bf16[8,192,256]{2,1,0:T(8,128)(2,1)S(1)}) fusion(bf16[1,24,8,8,256]{4,3,2,1,0:T(8,128)(2,1)S(1)} %copy-done, bf16[1,24,8,8,256]{4,3,2,1,0:T(8,128)(2,1)} %param.12), kind=kLoop, calls=%fused_computation | loop fusion | bytes 3145728 | tf_op jit(solution)/shard_map/reshape | solution.py:432
  46.6 0.1 copy-done.4
  46.7 0.0 copy-done.7
  46.7 18.4 %shard_map.148 = (bf16[8,192,256]{2,1,0:T(8,128)(2,1)S(1)}, f32[8,9,32,256]{3,2,1,0:T(8,128)}, f32[2,1536,128]{2,1,0:T(8,128)}, bf16[96,8,256]{2,1,0:T(8,128)(2,1)S(1)}, bf16[12,8,256]{2,1,0:T(8,128)(2,1)S(1)}) custom-call(s32[1]{0:T(128)} %bitcast.me_ref, s32[96]{0:T(128)S(1)} %reshape.58.links, s32[96]{0:T(128)S(1)} %reshape.59.codes, ...), custom_call_target="tpu_custom_call" | custom-call | tf_op jit(solution)/shard_map/pallas_call | solution.py:438
  65.1 0.9 copy-done.5
  66.6 0.0 copy-start.1
  66.6 1.7 %copy-done.1 = f32[8,9,32,256]{3,2,1,0:T(8,128)S(1)} copy-done((f32[8,9,32,256]{3,2,1,0:T(8,128)S(1)}, f32[8,9,32,256]{3,2,1,0:T(8,128)}, u32[]{:S(2)}) %copy-start.1) | copy-done | bytes 2359320
  68.3 46.0 %shard_map.149 = (f32[9,32,256]{2,1,0:T(8,128)S(1)}, bf16[8,40,8,256]{3,2,1,0:T(8,128)(2,1)S(1)}) custom-call(s32[28]{0:T(128)S(1)} %fusion.index, s32[1]{0:T(128)S(6)} %min.6.bit, f32[8,9,32,256]{3,2,1,0:T(8,128)S(1)} %copy-done.1, bf16[96,8,256]{2,1,0:T(8,128)(2,1)S(1)} %get-tuple-element.18.strips, bf16[12,8,256]{2,1,0:T(8,128)(2,1)S(1)} %get-tuple-element.19.corners, ...), custom_call_target="tpu_custom_call" | custom-call | tf_op jit(solution)/shard_map/pallas_call | solution.py:458
  114.3 3.5 %shard_map.150 = bf16[8,192,256]{2,1,0:T(8,128)(2,1)S(1)} custom-call(s32[1]{0:T(128)} %bitcast.me_ref, s32[96]{0:T(128)S(1)} %reshape.58.links, s32[96]{0:T(128)S(1)} %reshape.59.codes, s32[96]{0:T(128)S(1)} %reshape.60.corner_links, s32[96]{0:T(128)S(1)} %reshape.61.corner_codes, s32[768]{0:T(1024)S(1)} %copy-done.7, f32[2,1536,128]{2,1,0:T(8,128)S(1)} %copy-done.2, ...), custom_call_target="tpu_custom_call" | custom-call | tf_op jit(solution)/shard_map/pallas_call | solution.py:485
  117.7 0.0 copy-start.10
  117.7 1.0 copy_bitcast_fusion.1
  118.7 0.2 copy.94
  118.9 0.1 broadcast_in_dim_reshape.3
  119.0 0.0 copy-start.8
  119.7 0.8 multiply_add_fusion
  120.4 1.0 copy_bitcast_fusion.2
  (18 shorter events, 0.2 us)
Async XLA Ops:
  0.6 44.6 %copy-start = (bf16[1,24,8,8,256]{4,3,2,1,0:T(8,128)(2,1)S(1)}, bf16[1,24,8,8,256]{4,3,2,1,0:T(8,128)(2,1)}, u32[]{:S(2)}) copy-start(bf16[1,24,8,8,256]{4,3,2,1,0:T(8,128)(2,1)} %param.13) | copy-start | bytes 2359300
  2.5 1.0 copy-start.9
  2.7 41.5 %copy-start.11 = (s32[192,4]{0,1:T(4,128)S(1)}, s32[192,4]{0,1:T(4,128)}, u32[]{:S(2)}) copy-start(s32[192,4]{0,1:T(4,128)} %param.17) | copy-start | bytes 9220
  2.7 41.5 %copy-start.12 = (s32[192,4]{0,1:T(4,128)S(1)}, s32[192,4]{0,1:T(4,128)}, u32[]{:S(2)}) copy-start(s32[192,4]{0,1:T(4,128)} %param.16) | copy-start | bytes 9220
  2.7 42.0 %copy-start.13 = (s32[192,4]{0,1:T(4,128)S(1)}, s32[192,4]{0,1:T(4,128)}, u32[]{:S(2)}) copy-start(s32[192,4]{0,1:T(4,128)} %param.19) | copy-start | bytes 9220
  2.8 42.0 %copy-start.14 = (s32[192,4]{0,1:T(4,128)S(1)}, s32[192,4]{0,1:T(4,128)}, u32[]{:S(2)}) copy-start(s32[192,4]{0,1:T(4,128)} %param.18) | copy-start | bytes 9220
  43.2 1.1 copy-start.3
  45.2 1.5 %copy-start.4 = (bf16[8,9,32,256]{3,2,1,0:T(8,128)(2,1)S(1)}, bf16[8,9,32,256]{3,2,1,0:T(8,128)(2,1)}, u32[]{:S(2)}) copy-start(bf16[8,9,32,256]{3,2,1,0:T(8,128)(2,1)} %copy-done.3) | copy-start | bytes 3538948
  45.2 1.5 %copy-start.7 = (s32[768]{0:T(1024)S(1)}, s32[768]{0:T(1024)}, u32[]{:S(2)}) copy-start(s32[768]{0:T(1024)} %constant.33.clone.slots) | copy-start | bytes 9220
  65.1 0.9 copy-start.5
  66.6 1.7 %copy-start.1 = (f32[8,9,32,256]{3,2,1,0:T(8,128)S(1)}, f32[8,9,32,256]{3,2,1,0:T(8,128)}, u32[]{:S(2)}) copy-start(f32[8,9,32,256]{3,2,1,0:T(8,128)} %get-tuple-element.17.wgrad) | copy-start | bytes 7077892
  68.3 46.0 %copy-start.2 = (f32[2,1536,128]{2,1,0:T(8,128)S(1)}, f32[2,1536,128]{2,1,0:T(8,128)}, u32[]{:S(2)}) copy-start(f32[2,1536,128]{2,1,0:T(8,128)} %get-tuple-element.16.inner) | copy-start | bytes 4718596
  117.7 1.9 %copy-start.10 = (f32[1,288,256]{2,1,0:T(8,128)S(1)}, f32[1,288,256]{2,1,0:T(8,128)}, u32[]{:S(2)}) copy-start(f32[1,288,256]{2,1,0:T(8,128)} %param.15) | copy-start | bytes 884740
  118.7 1.7 %copy-start.6 = (bf16[8,192,256]{2,1,0:T(8,128)(2,1)S(1)}, bf16[8,192,256]{2,1,0:T(8,128)(2,1)}, u32[]{:S(2)}) copy-start(bf16[8,192,256]{2,1,0:T(8,128)(2,1)} %copy-done.5) | copy-start | bytes 2359300
  119.0 2.4 %copy-start.8 = (f32[1,288,256]{2,1,0:T(8,128)}, f32[1,288,256]{2,1,0:T(8,128)S(1)}, u32[]{:S(2)}) copy-start(f32[1,288,256]{2,1,0:T(8,128)S(1)} %broadcast_in_dim_reshape.3) | copy-start | bytes 884740

commit v3 on v2

--- a/solution.py
+++ b/solution.py
@@ -17,26 +17,48 @@
 LANES = 128
 
 
-def strip_lists(tiles, devices):
+def strip_lists(tiles, devices, side):
     sub = math.isqrt(tiles // 12)
     per = tiles // devices
     lists = [[] for _ in range(devices)]
     slot = np.full((tiles, 4), -1, np.int32)
+    end_slot = np.zeros((tiles, 4), np.int32)
+    end_row = np.zeros((tiles, 4), np.int32)
+
+    def split(tile):
+        return tile // (sub * sub), tile % (sub * sub) // sub, tile % sub
+
+    def near(tile, down, right):
+        face, row, col = split(tile)
+        r, c = row + down, col + right
+        inside = 0 <= r < sub and 0 <= c < sub
+        return inside and (face * sub * sub + r * sub + c) // per == tile // per
+
+    def add(tile, edge):
+        found = lists[tile // per]
+        slot[tile, edge] = len(found)
+        found.append(tile % per * 4 + edge)
+
     for tile in range(tiles):
-        face, row, col = tile // (sub * sub), tile % (sub * sub) // sub, tile % sub
-        owner = tile // per
         for edge, (down, right) in enumerate(((-1, 0), (1, 0), (0, -1), (0, 1))):
-            r, c = row + down, col + right
-            inside = 0 <= r < sub and 0 <= c < sub
-            if inside and (face * sub * sub + r * sub + c) // per == owner:
+            if not near(tile, down, right):
+                add(tile, edge)
+    for tile in range(tiles):
+        for q in range(4):
+            a, b = divmod(q, 2)
+            if near(tile, 2 * a - 1, 2 * b - 1):
                 continue
-            slot[tile, edge] = len(lists[owner])
-            lists[owner].append((tile - owner * per) * 4 + edge)
+            if slot[tile, a] < 0 and slot[tile, 2 + b] < 0:
+                add(tile, a)
+            if slot[tile, a] >= 0:
+                end_slot[tile, q], end_row[tile, q] = slot[tile, a], b * (side - 1)
+            else:
+                end_slot[tile, q], end_row[tile, q] = slot[tile, 2 + b], a * (side - 1)
     most = max(len(found) for found in lists)
     table = np.zeros((devices, most), np.int32)
     for owner, found in enumerate(lists):
         table[owner, : len(found)] = found
-    return most, table, np.maximum(slot, 0)
+    return most, table, np.maximum(slot, 0), end_slot, end_row
 
 
 def greet(peers):
@@ -73,22 +95,22 @@
 
 
 class Gather:
-    def __init__(self, n, src, dst, sends, recvs):
-        self.n, self.dst, self.sends, self.recvs = n, dst, sends, recvs
+    def __init__(self, n, src, dst, rows, sends, recvs):
+        self.n, self.dst, self.rows, self.sends, self.recvs = n, dst, rows, sends, recvs
         me = lax.axis_index("tile")
         self.me = me
         self.mate = {"tile": me + 1 - 2 * lax.rem(me, 2)}
         self.first = []
         for k in range(1, n // 2):
             peer = {"tile": lax.rem(me + 2 * k, n)}
-            self.first.append(send(src, dst.at[me], sends.at[k - 1], recvs.at[k - 1], peer))
+            self.first.append(send(src, dst.at[me, rows], sends.at[k - 1], recvs.at[k - 1], peer))
         at = n // 2 - 1
-        self.rest = [send(src, dst.at[me], sends.at[at], recvs.at[at], self.mate)]
+        self.rest = [send(src, dst.at[me, rows], sends.at[at], recvs.at[at], self.mate)]
 
     def forward(self):
         for k, copy in enumerate(self.first):
             copy.wait_recv()
-            block = self.dst.at[lax.rem(self.me + self.n - 2 * (k + 1), self.n)]
+            block = self.dst.at[lax.rem(self.me + self.n - 2 * (k + 1), self.n), self.rows]
             at = self.n // 2 + k
             self.rest.append(send(block, block, self.sends.at[at], self.recvs.at[at], self.mate))
 
@@ -99,16 +121,26 @@
             copy.wait()
 
 
-def gather_kernel(n, count, index, taps, strips, corners, all_taps, all_pack, pack, s1, r1, s2, r2):
+def gather_kernel(n, count, index, taps, strips, all_taps, all_pack, pack, *sems):
     greet(tile_peers(n))
-    one = Gather(n, taps, all_taps, s1, r1)
-    pack_strips(index, strips, corners, pack, count)
-    two = Gather(n, pack, all_pack, s2, r2)
-    all_taps[lax.axis_index("tile")] = taps[...]
-    one.forward()
-    two.forward()
-    one.finish()
-    two.finish()
+    me = lax.axis_index("tile")
+    parts = []
+    for c in range(3):
+        rows = pl.ds(3 * c, 3)
+        parts.append(Gather(n, taps.at[rows], all_taps, rows, *sems[2 * c : 2 * c + 2]))
+
+    @pl.loop(0, count)
+    def _(k):
+        pack[k] = strips[index[k]]
+
+    cut = count // 2
+    for c, rows in enumerate((pl.ds(0, cut), pl.ds(cut, count - cut))):
+        parts.append(Gather(n, pack.at[rows], all_pack, rows, *sems[2 * c + 6 : 2 * c + 8]))
+    all_taps[me] = taps[...]
+    for part in parts:
+        part.forward()
+    for part in parts:
+        part.finish()
 
 
 STEPS = 32000.0
@@ -149,6 +181,24 @@
     own = strips[here].astype(jnp.float32)
     other = all_pack[owner, slots[link * 4 + code]].astype(jnp.float32)
     return jnp.where(owner == me, own, other)
+
+
+def find_end(refs, ends, strips, all_pack, t, q):
+    me_ref, _, _, corner_links, corner_codes, _ = refs
+    end_slot, end_row = ends
+    per, side = strips.shape[0] // 4, strips.shape[1]
+    at = t * 4 + q
+    link, code = corner_links[at], corner_codes[at]
+    me = me_ref[0]
+    safe = jnp.maximum(link, 0)
+    owner = safe // per
+    own = strips[(safe - owner * per) * 4 + code // 2].astype(jnp.float32)
+    other = all_pack[owner, end_slot[safe * 4 + code]].astype(jnp.float32)
+    rows = jnp.where(owner == me, own, other)
+    row = jnp.where(owner == me, lax.rem(code, 2) * (side - 1), end_row[safe * 4 + code])
+    chosen = lax.broadcasted_iota(jnp.int32, rows.shape, 0) == row
+    chosen = chosen & (link >= 0)
+    return jnp.sum(jnp.where(chosen, rows, 0.0), axis=0, keepdims=True)
 
 
 def find_corner(refs, corners, all_pack, count, t, q):
@@ -170,12 +220,13 @@
 
 
 def main_kernel(
-    n, count, me_ref, links, codes, corner_links, corner_codes, slots,
-    fields, cot, all_taps, all_pack, strips, corners,
-    act, wgrad, inner, side_out, corner_out,
-    e0, e1, e2, x0, x1, x2, kern, dpre, d0, d1, d2,
+    n, me_ref, links, codes, corner_links, corner_codes, slots, end_slot, end_row,
+    fields, cot, all_taps, all_pack, strips,
+    act, wgrad, kern, dpre,
+    e0, e1, e2, x0, x1, x2,
 ):
     refs = (me_ref, links, codes, corner_links, corner_codes, slots)
+    ends = (end_slot, end_row)
     side, wide = fields.shape[0], fields.shape[1]
     per = wide // side
     rc = all_taps.shape[2]
@@ -204,10 +255,10 @@
         end = (side + 1) * wide + at
         put(e0, pl.ds(wide + at, side, stride=wide), find_strip(refs, strips, all_pack, t, 2))
         put(e2, pl.ds(wide + at + side - 1, side, stride=wide), find_strip(refs, strips, all_pack, t, 3))
-        put(e0, pl.ds(at, 1), find_corner(refs, corners, all_pack, count, t, 0))
-        put(e2, pl.ds(at + side - 1, 1), find_corner(refs, corners, all_pack, count, t, 1))
-        put(e0, pl.ds(end, 1), find_corner(refs, corners, all_pack, count, t, 2))
-        put(e2, pl.ds(end + side - 1, 1), find_corner(refs, corners, all_pack, count, t, 3))
+        put(e0, pl.ds(at, 1), find_end(refs, ends, strips, all_pack, t, 0))
+        put(e2, pl.ds(at + side - 1, 1), find_end(refs, ends, strips, all_pack, t, 1))
+        put(e0, pl.ds(end, 1), find_end(refs, ends, strips, all_pack, t, 2))
+        put(e2, pl.ds(end + side - 1, 1), find_end(refs, ends, strips, all_pack, t, 3))
 
     for x, e in ((x0, e0), (x1, e1), (x2, e2)):
         for half in range(e.shape[0]):
@@ -240,6 +291,12 @@
         )
         for owner in range(n):
             wgrad[owner, tap] = part[owner * rc : (owner + 1) * rc]
+
+
+def back_field(kern, dpre, inner, side_out, corner_out, d0, d1, d2):
+    f32 = jnp.float32
+    per, side = side_out.shape[0] // 4, side_out.shape[1]
+    wide = per * side
 
     @pl.loop(0, side + 2)
     def _(i):
@@ -282,9 +339,9 @@
 
 
 def reduce_kernel(
-    n, count, levels, total_count, index, bit, wgrad, strips, corners, weights,
-    averaged, all_pack,
-    pack, out_y, out_ys, in_y, in_ys, out_z, out_zs, in_z, in_zs, sums, updated, partner,
+    n, count, levels, total_count, index, bit, wgrad, kern, dpre, weights,
+    averaged, all_pack, inner, strips, corners,
+    d0, d1, d2, pack, out_y, out_ys, in_y, in_ys, out_z, out_zs, in_z, in_zs, sums, updated, partner,
     s1, r1, s2, r2, s3, r3, s4, r4, s5, r5, s6, r6, s7, r7,
 ):
     me = lax.axis_index("tile")
@@ -307,8 +364,12 @@
             send(out_y.at[k], in_y.at[k], s1.at[k], r1.at[k], mate),
             send(out_ys.at[k], in_ys.at[k], s2.at[k], r2.at[k], mate),
         )
+    back_field(kern, dpre, inner, strips, corners, d0, d1, d2)
     pack_strips(index, strips, corners, pack, count)
-    halo = Gather(n, pack, all_pack, s7, r7)
+    cut = pack.shape[0] // 2
+    halo = []
+    for c, rows in enumerate((pl.ds(0, cut), pl.ds(cut, pack.shape[0] - cut))):
+        halo.append(Gather(n, pack.at[rows], all_pack, rows, s7.at[c], r7.at[c]))
     grad = None
     for k in order:
         for copy in near[k]:
@@ -322,7 +383,8 @@
                 send(out_z.at[k - 1], in_z.at[k - 1], s3.at[k - 1], r3.at[k - 1], peer),
                 send(out_zs.at[k - 1], in_zs.at[k - 1], s4.at[k - 1], r4.at[k - 1], peer),
             )
-    halo.forward()
+    for part in halo:
+        part.forward()
     for k in far:
         for copy in far[k]:
             copy.wait()
@@ -344,7 +406,8 @@
     for copy in swaps:
         copy.wait()
     averaged[...] = 0.5 * (updated[...] + partner[bit[0]])
-    halo.finish()
+    for part in halo:
+        part.finish()
 
 
 def finish_kernel(
@@ -386,7 +449,7 @@
     line = n // 2
     levels = lax.axis_size("rep").bit_length() - 1
     me = lax.axis_index("tile")
-    count, table, slot_table = strip_lists(tile_links.shape[0], n)
+    count, table, slot_table, end_slot, end_row = strip_lists(tile_links.shape[0], n, side)
     rows = weights.shape[1]
     rc = rows // 9
     bf16, f32 = jnp.bfloat16, jnp.float32
@@ -409,22 +472,21 @@
     taps = (w_tap * total_count_scale(channels)).astype(bf16)
     strips = jnp.stack([block[:, 0], block[:, -1], block[:, :, 0], block[:, :, -1]], axis=1)
     strips = strips.reshape(per * 4, side, channels)
-    cells = jnp.stack(
-        [block[:, 0, 0], block[:, 0, -1], block[:, -1, 0], block[:, -1, -1]], axis=1
-    ).reshape(per // 2, 8, channels)
+    ends = (jnp.asarray(end_slot.reshape(-1)), jnp.asarray(end_row.reshape(-1)))
 
     params = functools.partial(pltpu.CompilerParams, vmem_limit_bytes=LIMIT)
     sems = [pltpu.SemaphoreType.DMA((n - 1,))] * 2
-    pack_shape = pltpu.VMEM((blocks, side, channels), bf16)
-    all_pack_shape = jax.ShapeDtypeStruct((n, blocks, side, channels), bf16)
     all_taps, all_pack = pl.pallas_call(
         functools.partial(gather_kernel, n, count),
-        out_shape=(jax.ShapeDtypeStruct((n, 9, rc, channels), bf16), all_pack_shape),
-        in_specs=[SMEM, VMEM, VMEM, VMEM],
+        out_shape=(
+            jax.ShapeDtypeStruct((n, 9, rc, channels), bf16),
+            jax.ShapeDtypeStruct((n, count, side, channels), bf16),
+        ),
+        in_specs=[SMEM, VMEM, VMEM],
         out_specs=(VMEM, VMEM),
-        scratch_shapes=[pack_shape] + sems * 2,
+        scratch_shapes=[pltpu.VMEM((count, side, channels), bf16)] + sems * 5,
         compiler_params=params(collective_id=0, has_side_effects=True),
-    )(index, taps, strips, cells)
+    )(index, taps, strips)
 
     wide = per * side
 
@@ -435,33 +497,36 @@
         return value.reshape(side, per, side, channels).transpose(1, 0, 2, 3)[None]
 
     tall = (side + 2) * wide
-    act, wgrad, inner, side_grads, corner_grads = pl.pallas_call(
-        functools.partial(main_kernel, n, count),
+    act, wgrad, kern, dpre = pl.pallas_call(
+        functools.partial(main_kernel, n),
         out_shape=(
             jax.ShapeDtypeStruct((side, wide, channels), bf16),
             jax.ShapeDtypeStruct((n, 9, rc, channels), f32),
+            jax.ShapeDtypeStruct((9, channels, channels), bf16),
+            jax.ShapeDtypeStruct(((side + 4) * wide, channels), bf16),
+        ),
+        in_specs=[SMEM] * 8 + [VMEM] * 5,
+        out_specs=(VMEM,) * 4,
+        scratch_shapes=[pltpu.VMEM((channels // LANES, tall, LANES), f32)] * 3
+        + [pltpu.VMEM((tall, channels), bf16)] * 3,
+        compiler_params=params(),
+    )(*tables, *ends, by_row(block), by_row(cotangent[0]), all_taps, all_pack, strips)
+
+    bit = jnp.clip(gossip_bit, 0, levels - 1)
+    averaged, all_back, inner, side_grads, corner_grads = pl.pallas_call(
+        functools.partial(reduce_kernel, n, count, levels, total_count),
+        out_shape=(
+            jax.ShapeDtypeStruct((9, rc, channels), f32),
+            jax.ShapeDtypeStruct((n, blocks, side, channels), bf16),
             jax.ShapeDtypeStruct((channels // LANES, side * wide, LANES), f32),
             jax.ShapeDtypeStruct((per * 4, side, channels), bf16),
             jax.ShapeDtypeStruct((per // 2, 8, channels), bf16),
         ),
-        in_specs=[SMEM] * 6 + [VMEM] * 6,
+        in_specs=[SMEM, SMEM, VMEM, VMEM, VMEM, VMEM],
         out_specs=(VMEM,) * 5,
         scratch_shapes=[pltpu.VMEM((channels // LANES, tall, LANES), f32)] * 3
-        + [pltpu.VMEM((tall, channels), bf16)] * 3
-        + [pltpu.VMEM((9, channels, channels), bf16)]
-        + [pltpu.VMEM(((side + 4) * wide, channels), bf16)]
-        + [pltpu.VMEM((channels // LANES, tall, LANES), f32)] * 3,
-        compiler_params=params(),
-    )(*tables, by_row(block), by_row(cotangent[0]), all_taps, all_pack, strips, cells)
-
-    bit = jnp.clip(gossip_bit, 0, levels - 1)
-    averaged, all_back = pl.pallas_call(
-        functools.partial(reduce_kernel, n, count, levels, total_count),
-        out_shape=(jax.ShapeDtypeStruct((9, rc, channels), f32), all_pack_shape),
-        in_specs=[SMEM, SMEM, VMEM, VMEM, VMEM, VMEM],
-        out_specs=(VMEM, VMEM),
-        scratch_shapes=[
-            pack_shape,
+        + [
+            pltpu.VMEM((blocks, side, channels), bf16),
             pltpu.VMEM((line, 9, rc, channels), jnp.int16),
             pltpu.VMEM((line, 9, 1, channels), f32),
             pltpu.VMEM((line, 9, rc, channels), jnp.int16),
@@ -478,9 +543,9 @@
         + [pltpu.SemaphoreType.DMA((line - 1,))] * 4
         + sems
         + [pltpu.SemaphoreType.DMA((levels,))] * 2
-        + sems,
+        + [pltpu.SemaphoreType.DMA((2, n - 1))] * 2,
         compiler_params=params(collective_id=1, has_side_effects=True),
-    )(index, bit, wgrad, side_grads, corner_grads, w_tap)
+    )(index, bit, wgrad, kern, dpre, w_tap)
 
     grads = pl.pallas_call(
         functools.partial(finish_kernel, count),

time: 122 us -> 116 us (0.951)
  Pallas kernels: 107 us -> 103 us
  local copies, waits for them, and re-layouts: 10.9 us -> 9.41 us
    pallas_call x1, Pallas kernels: 18.4 us -> 12.5 us  [body(): pl.pallas_call(functools.partial(main_kernel, n), out_shape=(jax.ShapeDty...]
    pallas_call x1, Pallas kernels: 46 us -> 51.6 us  [body(): pl.pallas_call(functools.partial(reduce_kernel, n, count, levels, total_c...]
    pallas_call x1, Pallas kernels: 39.5 us -> 35.5 us  [body(): pl.pallas_call(functools.partial(gather_kernel, n, count), out_shape=(jax...]
    reshape x1, local copies, waits for them, and re-layouts: 1.38 us -> 0.15 us  [by_row(): return value.transpose(1, 0, 2, 3).reshape(side, wide, channels)]
    unnamed x33 -> x29, local copies, waits for them, and re-layouts: 5.13 us -> 4.94 us
where the time goes in v3:
time: 116 us
  Pallas kernels  103 us (89%)
  local copies, waits for them, and re-layouts  9.41 us (8%)
  between operations  2.25 us (2%)
    pallas_call x1, Pallas kernels, body(): pl.pallas_call(functools.partial(reduce_kernel, n, count, levels, total_c...  51.6 us
    pallas_call x1, Pallas kernels, body(): pl.pallas_call(functools.partial(gather_kernel, n, count), out_shape=(jax...  35.5 us
    pallas_call x1, Pallas kernels, body(): pl.pallas_call(functools.partial(main_kernel, n), out_shape=(jax.ShapeDty...  12.5 us
    unnamed x29, local copies, waits for them, and re-layouts  4.94 us
    pallas_call x1, Pallas kernels, body(): pl.pallas_call(functools.partial(finish_kernel, count), out_shape=jax.Sha...  3.46 us

profile of v3, /device:TPU:0, one launch (start us, length us, event | category | flops | bytes accessed | tf_op | source)
XLA Modules:
  0.0 115.7 jit_solution(14381014662592994383)
XLA Ops:
  0.6 0.0 copy-start
  0.6 0.8 fusion.index
  1.4 1.3 %copy.52 = bf16[1,24,8,8,256]{4,2,1,3,0:T(8,128)(2,1)S(1)} copy(bf16[1,24,8,8,256]{4,3,2,1,0:T(8,128)(2,1)} %param.14) | data formatting | bytes 1572864 | tf_op args[0]
  2.7 0.3 fusion.1
  3.0 0.0 copy-start.8
  3.0 0.1 copy.38
  3.1 0.1 copy.39
  3.1 0.1 pad_maximum_fusion
  3.2 0.0 copy-start.10
  3.3 0.0 copy-start.11
  3.3 0.0 copy-start.12
  3.3 0.0 copy-start.13
  3.3 0.0 copy-start.6
  3.3 0.6 copy-done.8
  4.0 0.2 multiply_convert_fusion
  4.2 35.5 %shard_map.165 = (bf16[8,9,32,256]{3,2,1,0:T(8,128)(2,1)S(1)}, bf16[8,28,8,256]{3,2,1,0:T(8,128)(2,1)S(1)}) custom-call(s32[28]{0:T(128)S(1)} %fusion.index, bf16[9,32,256]{2,1,0:T(8,128)(2,1)S(1)} %get-tuple-element.26.taps, bf16[96,8,256]{2,1,0:T(8,128)(2,1)S(1)} %bitcast.43), custom_call_target="tpu_custom_call" | custom-call | tf_op jit(solution)/shard_map/pallas_call | solution.py:479
  39.7 0.0 copy-start.2
  39.7 1.0 copy-done.2
  40.8 0.0 copy-done.10
  40.8 0.0 copy-done.11
  40.8 0.1 constant_dynamic-slice_fusion.3
  40.8 0.1 copy.30
  40.9 0.1 reshape.55.links
  41.0 0.1 copy.31
  41.1 0.1 reshape.56.codes
  41.2 0.1 constant_dynamic-slice_fusion.1
  41.3 0.1 copy.32
  41.4 0.1 reshape.57.corner_links
  41.5 0.1 copy.33
  41.6 0.1 reshape.58.corner_codes
  41.7 0.0 copy-start.3
  41.7 0.0 copy-start.4
  41.7 0.0 copy-start.5
  41.7 0.2 copy_bitcast_fusion
  41.9 0.5 copy-done.3
  42.4 0.0 copy-done.4
  42.4 0.0 copy-done.5
  42.4 12.5 %shard_map.166 = (bf16[8,192,256]{2,1,0:T(8,128)(2,1)S(1)}, f32[8,9,32,256]{3,2,1,0:T(8,128)}, bf16[9,256,256]{2,1,0:T(8,128)(2,1)S(1)}, bf16[2304,256]{1,0:T(8,128)(2,1)S(1)}) custom-call(s32[1]{0:T(128)} %bitcast.me_ref, s32[96]{0:T(128)S(1)} %reshape.55.links, s32[96]{0:T(128)S(1)} %reshape.56.codes, s32[96]{0:T(128)S(1)} %reshape.57.corner_links, ...), custom_call_target="tpu_custom_call" | custom-call | tf_op jit(solution)/shard_map/pallas_call | solution.py:500
  55.5 51.6 %shard_map.167 = (f32[9,32,256]{2,1,0:T(8,128)S(1)}, bf16[8,40,8,256]{3,2,1,0:T(8,128)(2,1)S(1)}, f32[2,1536,128]{2,1,0:T(8,128)}, bf16[96,8,256]{2,1,0:T(8,128)(2,1)S(1)}, bf16[12,8,256]{2,1,0:T(8,128)(2,1)S(1)}) custom-call(s32[28]{0:T(128)S(1)} %fusion.index, s32[1]{0:T(128)S(6)} %min.6.bit, f32[8,9,32,256]{3,2,1,0:T(8,128)} %get-tuple-element.18.wgrad, ...), custom_call_target="tpu_custom_call" | custom-call | tf_op jit(solution)/shard_map/pallas_call | solution.py:516
  107.2 1.4 %copy-done.1 = f32[2,1536,128]{2,1,0:T(8,128)S(1)} copy-done((f32[2,1536,128]{2,1,0:T(8,128)S(1)}, f32[2,1536,128]{2,1,0:T(8,128)}, u32[]{:S(2)}) %copy-start.1) | copy-done | bytes 1572888
  108.6 3.5 %shard_map.168 = bf16[8,192,256]{2,1,0:T(8,128)(2,1)S(1)} custom-call(s32[1]{0:T(128)} %bitcast.me_ref, s32[96]{0:T(128)S(1)} %reshape.55.links, s32[96]{0:T(128)S(1)} %reshape.56.codes, s32[96]{0:T(128)S(1)} %reshape.57.corner_links, s32[96]{0:T(128)S(1)} %reshape.58.corner_codes, s32[768]{0:T(1024)S(1)} %copy-done.3, f32[2,1536,128]{2,1,0:T(8,128)S(1)} %copy-done.1, ...), custom_call_target="tpu_custom_call" | custom-call | tf_op jit(solution)/shard_map/pallas_call | solution.py:550
  112.0 0.0 copy-start.9
  112.0 1.0 copy_bitcast_fusion.1
  113.0 0.2 copy.43
  113.2 0.1 broadcast_in_dim_reshape.3
  113.3 0.0 copy-start.7
  114.0 0.8 multiply_add_fusion
  114.7 1.0 copy_bitcast_fusion.2
  (10 shorter events, 0.1 us)
Async XLA Ops:
  0.6 41.1 %copy-start = (bf16[1,24,8,8,256]{4,3,2,1,0:T(8,128)(2,1)S(1)}, bf16[1,24,8,8,256]{4,3,2,1,0:T(8,128)(2,1)}, u32[]{:S(2)}) copy-start(bf16[1,24,8,8,256]{4,3,2,1,0:T(8,128)(2,1)} %param.15) | copy-start | bytes 2359300
  3.0 1.0 copy-start.8
  3.2 37.5 %copy-start.10 = (s32[192,4]{0,1:T(4,128)S(1)}, s32[192,4]{0,1:T(4,128)}, u32[]{:S(2)}) copy-start(s32[192,4]{0,1:T(4,128)} %param.19) | copy-start | bytes 9220
  3.3 37.5 %copy-start.11 = (s32[192,4]{0,1:T(4,128)S(1)}, s32[192,4]{0,1:T(4,128)}, u32[]{:S(2)}) copy-start(s32[192,4]{0,1:T(4,128)} %param.18) | copy-start | bytes 9220
  3.3 37.9 %copy-start.12 = (s32[192,4]{0,1:T(4,128)S(1)}, s32[192,4]{0,1:T(4,128)}, u32[]{:S(2)}) copy-start(s32[192,4]{0,1:T(4,128)} %param.21) | copy-start | bytes 9220
  3.3 37.9 %copy-start.13 = (s32[192,4]{0,1:T(4,128)S(1)}, s32[192,4]{0,1:T(4,128)}, u32[]{:S(2)}) copy-start(s32[192,4]{0,1:T(4,128)} %param.20) | copy-start | bytes 9220
  3.3 38.4 %copy-start.6 = (bf16[1,24,8,8,256]{4,3,2,1,0:T(8,128)(2,1)S(1)}, bf16[1,24,8,8,256]{4,3,2,1,0:T(8,128)(2,1)}, u32[]{:S(2)}) copy-start(bf16[1,24,8,8,256]{4,3,2,1,0:T(8,128)(2,1)} %param.14) | copy-start | bytes 2359300
  39.7 1.0 copy-start.2
  41.7 0.7 copy-start.3
  41.7 0.7 copy-start.4
  41.7 0.7 copy-start.5
  107.2 1.4 %copy-start.1 = (f32[2,1536,128]{2,1,0:T(8,128)S(1)}, f32[2,1536,128]{2,1,0:T(8,128)}, u32[]{:S(2)}) copy-start(f32[2,1536,128]{2,1,0:T(8,128)} %get-tuple-element.21.inner) | copy-start | bytes 4718596
  112.0 1.9 %copy-start.9 = (f32[1,288,256]{2,1,0:T(8,128)S(1)}, f32[1,288,256]{2,1,0:T(8,128)}, u32[]{:S(2)}) copy-start(f32[1,288,256]{2,1,0:T(8,128)} %param.17) | copy-start | bytes 884740
  113.3 2.4 %copy-start.7 = (f32[1,288,256]{2,1,0:T(8,128)}, f32[1,288,256]{2,1,0:T(8,128)S(1)}, u32[]{:S(2)}) copy-start(f32[1,288,256]{2,1,0:T(8,128)S(1)} %broadcast_in_dim_reshape.3) | copy-start | bytes 884740

commit v4 on v3

--- a/solution.py
+++ b/solution.py
@@ -365,11 +365,6 @@
             send(out_ys.at[k], in_ys.at[k], s2.at[k], r2.at[k], mate),
         )
     back_field(kern, dpre, inner, strips, corners, d0, d1, d2)
-    pack_strips(index, strips, corners, pack, count)
-    cut = pack.shape[0] // 2
-    halo = []
-    for c, rows in enumerate((pl.ds(0, cut), pl.ds(cut, pack.shape[0] - cut))):
-        halo.append(Gather(n, pack.at[rows], all_pack, rows, s7.at[c], r7.at[c]))
     grad = None
     for k in order:
         for copy in near[k]:
@@ -383,8 +378,11 @@
                 send(out_z.at[k - 1], in_z.at[k - 1], s3.at[k - 1], r3.at[k - 1], peer),
                 send(out_zs.at[k - 1], in_zs.at[k - 1], s4.at[k - 1], r4.at[k - 1], peer),
             )
-    for part in halo:
-        part.forward()
+    pack_strips(index, strips, corners, pack, count)
+    cut = pack.shape[0] // 2
+    halo = []
+    for c, rows in enumerate((pl.ds(0, cut), pl.ds(cut, pack.shape[0] - cut))):
+        halo.append(Gather(n, pack.at[rows], all_pack, rows, s7.at[c], r7.at[c]))
     for k in far:
         for copy in far[k]:
             copy.wait()
@@ -396,6 +394,7 @@
     small = []
     for k, peer in enumerate(peers):
         small.append(send(sums.at[0], sums.at[k + 1], s5.at[k], r5.at[k], peer))
+    halo[0].forward()
     for copy in small:
         copy.wait()
     mean = jnp.sum(sums[...], keepdims=True) / total_count
@@ -403,6 +402,8 @@
     swaps = []
     for level, friend in enumerate(friends):
         swaps.append(send(updated, partner.at[level], s6.at[level], r6.at[level], friend))
+    for part in halo[1:]:
+        part.forward()
     for copy in swaps:
         copy.wait()
     averaged[...] = 0.5 * (updated[...] + partner[bit[0]])

time: 116 us -> 115 us (level)
    pallas_call x1, Pallas kernels: 51.6 us -> 50.1 us  [body(): pl.pallas_call(functools.partial(reduce_kernel, n, count, levels, total_c...]
where the time goes in v4:
time: 115 us; the launch traced here: 114 us
  Pallas kernels  102 us (89%)
  local copies, waits for them, and re-layouts  9.41 us (8%)
  between operations  2.25 us (2%)
    pallas_call x1, Pallas kernels, body(): pl.pallas_call(functools.partial(reduce_kernel, n, count, levels, total_c...  50.1 us
    pallas_call x1, Pallas kernels, body(): pl.pallas_call(functools.partial(gather_kernel, n, count), out_shape=(jax...  35.5 us
    pallas_call x1, Pallas kernels, body(): pl.pallas_call(functools.partial(main_kernel, n), out_shape=(jax.ShapeDty...  12.5 us
    unnamed x29, local copies, waits for them, and re-layouts  4.94 us
    pallas_call x1, Pallas kernels, body(): pl.pallas_call(functools.partial(finish_kernel, count), out_shape=jax.Sha...  3.46 us

profile of v4, /device:TPU:0, one launch (start us, length us, event | category | flops | bytes accessed | tf_op | source)
XLA Modules:
  0.0 114.2 jit_solution(11083895003015717611)
XLA Ops:
  0.6 0.0 copy-start
  0.6 0.8 fusion.index
  1.4 1.3 %copy.52 = bf16[1,24,8,8,256]{4,2,1,3,0:T(8,128)(2,1)S(1)} copy(bf16[1,24,8,8,256]{4,3,2,1,0:T(8,128)(2,1)} %param.14) | data formatting | bytes 1572864 | tf_op args[0]
  2.7 0.3 fusion.1
  3.0 0.0 copy-start.8
  3.0 0.1 copy.38
  3.1 0.1 copy.39
  3.1 0.1 pad_maximum_fusion
  3.2 0.0 copy-start.10
  3.3 0.0 copy-start.11
  3.3 0.0 copy-start.12
  3.3 0.0 copy-start.13
  3.3 0.0 copy-start.6
  3.3 0.6 copy-done.8
  4.0 0.2 multiply_convert_fusion
  4.2 35.5 %shard_map.165 = (bf16[8,9,32,256]{3,2,1,0:T(8,128)(2,1)S(1)}, bf16[8,28,8,256]{3,2,1,0:T(8,128)(2,1)S(1)}) custom-call(s32[28]{0:T(128)S(1)} %fusion.index, bf16[9,32,256]{2,1,0:T(8,128)(2,1)S(1)} %get-tuple-element.26.taps, bf16[96,8,256]{2,1,0:T(8,128)(2,1)S(1)} %bitcast.43), custom_call_target="tpu_custom_call" | custom-call | tf_op jit(solution)/shard_map/pallas_call | solution.py:480
  39.7 1.0 copy-done.2
  40.8 0.0 copy-done.11
  40.8 0.1 constant_dynamic-slice_fusion.3
  40.8 0.1 copy.30
  40.9 0.1 reshape.55.links
  41.0 0.1 copy.31
  41.1 0.1 reshape.56.codes
  41.2 0.0 copy-done.12
  41.2 0.0 copy-done.13
  41.2 0.1 constant_dynamic-slice_fusion.1
  41.3 0.1 copy.32
  41.4 0.1 reshape.57.corner_links
  41.5 0.1 copy.33
  41.6 0.1 reshape.58.corner_codes
  41.7 0.0 copy-start.3
  41.7 0.0 copy-start.4
  41.7 0.0 copy-start.5
  41.7 0.2 copy_bitcast_fusion
  41.9 0.5 copy-done.3
  42.4 0.0 copy-done.4
  42.4 0.0 copy-done.5
  42.4 12.5 %shard_map.166 = (bf16[8,192,256]{2,1,0:T(8,128)(2,1)S(1)}, f32[8,9,32,256]{3,2,1,0:T(8,128)}, bf16[9,256,256]{2,1,0:T(8,128)(2,1)S(1)}, bf16[2304,256]{1,0:T(8,128)(2,1)S(1)}) custom-call(s32[1]{0:T(128)} %bitcast.me_ref, s32[96]{0:T(128)S(1)} %reshape.55.links, s32[96]{0:T(128)S(1)} %reshape.56.codes, s32[96]{0:T(128)S(1)} %reshape.57.corner_links, ...), custom_call_target="tpu_custom_call" | custom-call | tf_op jit(solution)/shard_map/pallas_call | solution.py:501
  55.5 50.1 %shard_map.167 = (f32[9,32,256]{2,1,0:T(8,128)S(1)}, bf16[8,40,8,256]{3,2,1,0:T(8,128)(2,1)S(1)}, f32[2,1536,128]{2,1,0:T(8,128)}, bf16[96,8,256]{2,1,0:T(8,128)(2,1)S(1)}, bf16[12,8,256]{2,1,0:T(8,128)(2,1)S(1)}) custom-call(s32[28]{0:T(128)S(1)} %fusion.index, s32[1]{0:T(128)S(6)} %min.6.bit, f32[8,9,32,256]{3,2,1,0:T(8,128)} %get-tuple-element.18.wgrad, ...), custom_call_target="tpu_custom_call" | custom-call | tf_op jit(solution)/shard_map/pallas_call | solution.py:517
  105.7 1.4 %copy-done.1 = f32[2,1536,128]{2,1,0:T(8,128)S(1)} copy-done((f32[2,1536,128]{2,1,0:T(8,128)S(1)}, f32[2,1536,128]{2,1,0:T(8,128)}, u32[]{:S(2)}) %copy-start.1) | copy-done | bytes 1572888
  107.1 3.5 %shard_map.168 = bf16[8,192,256]{2,1,0:T(8,128)(2,1)S(1)} custom-call(s32[1]{0:T(128)} %bitcast.me_ref, s32[96]{0:T(128)S(1)} %reshape.55.links, s32[96]{0:T(128)S(1)} %reshape.56.codes, s32[96]{0:T(128)S(1)} %reshape.57.corner_links, s32[96]{0:T(128)S(1)} %reshape.58.corner_codes, s32[768]{0:T(1024)S(1)} %copy-done.3, f32[2,1536,128]{2,1,0:T(8,128)S(1)} %copy-done.1, ...), custom_call_target="tpu_custom_call" | custom-call | tf_op jit(solution)/shard_map/pallas_call | solution.py:551
  110.6 0.0 copy-start.9
  110.6 1.0 copy_bitcast_fusion.1
  111.6 0.2 copy.43
  111.7 0.1 broadcast_in_dim_reshape.3
  111.8 0.0 copy-start.7
  112.5 0.8 multiply_add_fusion
  113.3 1.0 copy_bitcast_fusion.2
  (10 shorter events, 0.1 us)
Async XLA Ops:
  0.6 41.1 %copy-start = (bf16[1,24,8,8,256]{4,3,2,1,0:T(8,128)(2,1)S(1)}, bf16[1,24,8,8,256]{4,3,2,1,0:T(8,128)(2,1)}, u32[]{:S(2)}) copy-start(bf16[1,24,8,8,256]{4,3,2,1,0:T(8,128)(2,1)} %param.15) | copy-start | bytes 2359300
  3.0 1.0 copy-start.8
  3.2 37.5 %copy-start.10 = (s32[192,4]{0,1:T(4,128)S(1)}, s32[192,4]{0,1:T(4,128)}, u32[]{:S(2)}) copy-start(s32[192,4]{0,1:T(4,128)} %param.19) | copy-start | bytes 9220
  3.3 37.5 %copy-start.11 = (s32[192,4]{0,1:T(4,128)S(1)}, s32[192,4]{0,1:T(4,128)}, u32[]{:S(2)}) copy-start(s32[192,4]{0,1:T(4,128)} %param.18) | copy-start | bytes 9220
  3.3 37.9 %copy-start.12 = (s32[192,4]{0,1:T(4,128)S(1)}, s32[192,4]{0,1:T(4,128)}, u32[]{:S(2)}) copy-start(s32[192,4]{0,1:T(4,128)} %param.21) | copy-start | bytes 9220
  3.3 37.9 %copy-start.13 = (s32[192,4]{0,1:T(4,128)S(1)}, s32[192,4]{0,1:T(4,128)}, u32[]{:S(2)}) copy-start(s32[192,4]{0,1:T(4,128)} %param.20) | copy-start | bytes 9220
  3.3 38.4 %copy-start.6 = (bf16[1,24,8,8,256]{4,3,2,1,0:T(8,128)(2,1)S(1)}, bf16[1,24,8,8,256]{4,3,2,1,0:T(8,128)(2,1)}, u32[]{:S(2)}) copy-start(bf16[1,24,8,8,256]{4,3,2,1,0:T(8,128)(2,1)} %param.14) | copy-start | bytes 2359300
  39.7 1.0 copy-start.2
  41.7 0.7 copy-start.3
  41.7 0.7 copy-start.4
  41.7 0.7 copy-start.5
  105.7 1.4 %copy-start.1 = (f32[2,1536,128]{2,1,0:T(8,128)S(1)}, f32[2,1536,128]{2,1,0:T(8,128)}, u32[]{:S(2)}) copy-start(f32[2,1536,128]{2,1,0:T(8,128)} %get-tuple-element.21.inner) | copy-start | bytes 4718596
  110.6 1.9 %copy-start.9 = (f32[1,288,256]{2,1,0:T(8,128)S(1)}, f32[1,288,256]{2,1,0:T(8,128)}, u32[]{:S(2)}) copy-start(f32[1,288,256]{2,1,0:T(8,128)} %param.17) | copy-start | bytes 884740
  111.8 2.4 %copy-start.7 = (f32[1,288,256]{2,1,0:T(8,128)}, f32[1,288,256]{2,1,0:T(8,128)S(1)}, u32[]{:S(2)}) copy-start(f32[1,288,256]{2,1,0:T(8,128)S(1)} %broadcast_in_dim_reshape.3) | copy-start | bytes 884740

commit v5 on v3

--- a/solution.py
+++ b/solution.py
@@ -222,8 +222,8 @@
 def main_kernel(
     n, me_ref, links, codes, corner_links, corner_codes, slots, end_slot, end_row,
     fields, cot, all_taps, all_pack, strips,
-    act, wgrad, kern, dpre,
-    e0, e1, e2, x0, x1, x2,
+    act, inner, side_out, corner_out, dpre, x0, x1, x2,
+    e0, e1, e2, kern, d0, d1, d2,
 ):
     refs = (me_ref, links, codes, corner_links, corner_codes, slots)
     ends = (end_slot, end_row)
@@ -281,16 +281,7 @@
         grad = cot[i].astype(f32) * (s * (1.0 + pre * (1.0 - s)))
         dpre[pl.ds(pl.multiple_of((i + 2) * wide, 16), wide)] = grad.astype(jnp.bfloat16)
 
-    for tap in range(9):
-        a, b = divmod(tap, 3)
-        part = lax.dot_general(
-            xs[b][a * wide : (a + side) * wide],
-            dpre[2 * wide : (side + 2) * wide],
-            (((0,), (0,)), ((), ())),
-            preferred_element_type=f32,
-        )
-        for owner in range(n):
-            wgrad[owner, tap] = part[owner * rc : (owner + 1) * rc]
+    back_field(kern, dpre, inner, side_out, corner_out, d0, d1, d2)
 
 
 def back_field(kern, dpre, inner, side_out, corner_out, d0, d1, d2):
@@ -338,10 +329,27 @@
         corner_out[pair] = jnp.concatenate(rows, axis=0).astype(jnp.bfloat16)
 
 
+def kernel_gradient(n, xs, dpre, wgrad):
+    f32 = jnp.float32
+    rc = wgrad.shape[2]
+    wide = (dpre.shape[0] - xs[0].shape[0]) // 2
+    side = dpre.shape[0] // wide - 4
+    for tap in range(9):
+        a, b = divmod(tap, 3)
+        part = lax.dot_general(
+            xs[b][a * wide : (a + side) * wide],
+            dpre[2 * wide : (side + 2) * wide],
+            (((0,), (0,)), ((), ())),
+            preferred_element_type=f32,
+        )
+        for owner in range(n):
+            wgrad[owner, tap] = part[owner * rc : (owner + 1) * rc]
+
+
 def reduce_kernel(
-    n, count, levels, total_count, index, bit, wgrad, kern, dpre, weights,
-    averaged, all_pack, inner, strips, corners,
-    d0, d1, d2, pack, out_y, out_ys, in_y, in_ys, out_z, out_zs, in_z, in_zs, sums, updated, partner,
+    n, count, levels, total_count, index, bit, x0, x1, x2, dpre, strips, corners, weights,
+    averaged, all_pack,
+    wgrad, pack, out_y, out_ys, in_y, in_ys, out_z, out_zs, in_z, in_zs, sums, updated, partner,
     s1, r1, s2, r2, s3, r3, s4, r4, s5, r5, s6, r6, s7, r7,
 ):
     me = lax.axis_index("tile")
@@ -352,6 +360,12 @@
         step = 2**level
         friends.append({"rep": rep + step * (1 - 2 * lax.rem(rep // step, 2))})
     greet(peers + friends)
+    pack_strips(index, strips, corners, pack, count)
+    cut = pack.shape[0] // 2
+    halo = []
+    for c, rows in enumerate((pl.ds(0, cut), pl.ds(cut, pack.shape[0] - cut))):
+        halo.append(Gather(n, pack.at[rows], all_pack, rows, s7.at[c], r7.at[c]))
+    kernel_gradient(n, (x0, x1, x2), dpre, wgrad)
     line = n // 2
     odd = lax.rem(me, 2)
     mate = {"tile": me + 1 - 2 * odd}
@@ -364,12 +378,6 @@
             send(out_y.at[k], in_y.at[k], s1.at[k], r1.at[k], mate),
             send(out_ys.at[k], in_ys.at[k], s2.at[k], r2.at[k], mate),
         )
-    back_field(kern, dpre, inner, strips, corners, d0, d1, d2)
-    pack_strips(index, strips, corners, pack, count)
-    cut = pack.shape[0] // 2
-    halo = []
-    for c, rows in enumerate((pl.ds(0, cut), pl.ds(cut, pack.shape[0] - cut))):
-        halo.append(Gather(n, pack.at[rows], all_pack, rows, s7.at[c], r7.at[c]))
     grad = None
     for k in order:
         for copy in near[k]:
@@ -497,35 +505,38 @@
         return value.reshape(side, per, side, channels).transpose(1, 0, 2, 3)[None]
 
     tall = (side + 2) * wide
-    act, wgrad, kern, dpre = pl.pallas_call(
+    flat = jax.ShapeDtypeStruct((tall, channels), bf16)
+    act, inner, side_grads, corner_grads, dpre, x0, x1, x2 = pl.pallas_call(
         functools.partial(main_kernel, n),
         out_shape=(
             jax.ShapeDtypeStruct((side, wide, channels), bf16),
-            jax.ShapeDtypeStruct((n, 9, rc, channels), f32),
-            jax.ShapeDtypeStruct((9, channels, channels), bf16),
+            jax.ShapeDtypeStruct((channels // LANES, side * wide, LANES), f32),
+            jax.ShapeDtypeStruct((per * 4, side, channels), bf16),
+            jax.ShapeDtypeStruct((per // 2, 8, channels), bf16),
             jax.ShapeDtypeStruct(((side + 4) * wide, channels), bf16),
+            flat,
+            flat,
+            flat,
         ),
         in_specs=[SMEM] * 8 + [VMEM] * 5,
-        out_specs=(VMEM,) * 4,
+        out_specs=(VMEM,) * 8,
         scratch_shapes=[pltpu.VMEM((channels // LANES, tall, LANES), f32)] * 3
-        + [pltpu.VMEM((tall, channels), bf16)] * 3,
+        + [pltpu.VMEM((9, channels, channels), bf16)]
+        + [pltpu.VMEM((channels // LANES, tall, LANES), f32)] * 3,
         compiler_params=params(),
     )(*tables, *ends, by_row(block), by_row(cotangent[0]), all_taps, all_pack, strips)
 
     bit = jnp.clip(gossip_bit, 0, levels - 1)
-    averaged, all_back, inner, side_grads, corner_grads = pl.pallas_call(
+    averaged, all_back = pl.pallas_call(
         functools.partial(reduce_kernel, n, count, levels, total_count),
         out_shape=(
             jax.ShapeDtypeStruct((9, rc, channels), f32),
             jax.ShapeDtypeStruct((n, blocks, side, channels), bf16),
-            jax.ShapeDtypeStruct((channels // LANES, side * wide, LANES), f32),
-            jax.ShapeDtypeStruct((per * 4, side, channels), bf16),
-            jax.ShapeDtypeStruct((per // 2, 8, channels), bf16),
         ),
-        in_specs=[SMEM, SMEM, VMEM, VMEM, VMEM, VMEM],
-        out_specs=(VMEM,) * 5,
-        scratch_shapes=[pltpu.VMEM((channels // LANES, tall, LANES), f32)] * 3
-        + [
+        in_specs=[SMEM, SMEM] + [VMEM] * 7,
+        out_specs=(VMEM,) * 2,
+        scratch_shapes=[
+            pltpu.VMEM((n, 9, rc, channels), f32),
             pltpu.VMEM((blocks, side, channels), bf16),
             pltpu.VMEM((line, 9, rc, channels), jnp.int16),
             pltpu.VMEM((line, 9, 1, channels), f32),
@@ -545,7 +556,7 @@
         + [pltpu.SemaphoreType.DMA((levels,))] * 2
         + [pltpu.SemaphoreType.DMA((2, n - 1))] * 2,
         compiler_params=params(collective_id=1, has_side_effects=True),
-    )(index, bit, wgrad, kern, dpre, w_tap)
+    )(index, bit, x0, x1, x2, dpre, side_grads, corner_grads, w_tap)
 
     grads = pl.pallas_call(
         functools.partial(finish_kernel, count),

time: 116 us -> 115 us (level)
  Pallas kernels: 103 us -> 99.8 us
  local copies, waits for them, and re-layouts: 9.41 us -> 11.8 us
    pallas_call x1, Pallas kernels: 51.6 us -> 43.8 us  [body(): pl.pallas_call(functools.partial(reduce_kernel, n, count, levels, total_c...]
    pallas_call x1, Pallas kernels: 12.5 us -> 17.1 us  [body(): pl.pallas_call(functools.partial(main_kernel, n), out_shape=(jax.ShapeDty...]
    unnamed x29 -> x35, local copies, waits for them, and re-layouts: 4.94 us -> 7.31 us
where the time goes in v5:
time: 115 us
  Pallas kernels  99.8 us (87%)
  local copies, waits for them, and re-layouts  11.8 us (10%)
  between operations  2.27 us (2%)
    pallas_call x1, Pallas kernels, body(): pl.pallas_call(functools.partial(reduce_kernel, n, count, levels, total_c...  43.8 us
    pallas_call x1, Pallas kernels, body(): pl.pallas_call(functools.partial(gather_kernel, n, count), out_shape=(jax...  35.5 us
    pallas_call x1, Pallas kernels, body(): pl.pallas_call(functools.partial(main_kernel, n), out_shape=(jax.ShapeDty...  17.1 us
    unnamed x35, local copies, waits for them, and re-layouts  7.31 us
    pallas_call x1, Pallas kernels, body(): pl.pallas_call(functools.partial(finish_kernel, count), out_shape=jax.Sha...  3.46 us

profile of v5, /device:TPU:0, one launch (start us, length us, event | category | flops | bytes accessed | tf_op | source)
XLA Modules:
  0.0 114.9 jit_solution(11307786346352840481)
XLA Ops:
  0.6 0.0 copy-start
  0.6 0.8 fusion.index
  1.4 1.3 %copy.52 = bf16[1,24,8,8,256]{4,2,1,3,0:T(8,128)(2,1)S(1)} copy(bf16[1,24,8,8,256]{4,3,2,1,0:T(8,128)(2,1)} %param.14) | data formatting | bytes 1572864 | tf_op args[0]
  2.7 0.3 fusion.1
  3.0 0.0 copy-start.11
  3.0 0.1 copy.38
  3.1 0.1 copy.39
  3.1 0.1 pad_maximum_fusion
  3.2 0.0 copy-start.13
  3.3 0.0 copy-start.14
  3.3 0.0 copy-start.15
  3.3 0.0 copy-start.16
  3.3 0.0 copy-start.9
  3.3 0.6 copy-done.11
  4.0 0.2 multiply_convert_fusion
  4.2 35.5 %shard_map.165 = (bf16[8,9,32,256]{3,2,1,0:T(8,128)(2,1)S(1)}, bf16[8,28,8,256]{3,2,1,0:T(8,128)(2,1)S(1)}) custom-call(s32[28]{0:T(128)S(1)} %fusion.index, bf16[9,32,256]{2,1,0:T(8,128)(2,1)S(1)} %get-tuple-element.28.taps, bf16[96,8,256]{2,1,0:T(8,128)(2,1)S(1)} %bitcast.43), custom_call_target="tpu_custom_call" | custom-call | tf_op jit(solution)/shard_map/pallas_call | solution.py:487
  39.7 0.0 copy-start.3
  39.7 1.0 copy-done.3
  40.8 0.1 constant_dynamic-slice_fusion.3
  40.8 0.1 copy.30
  40.9 0.1 reshape.55.links
  41.0 0.1 copy.31
  41.1 0.1 reshape.56.codes
  41.2 0.1 constant_dynamic-slice_fusion.1
  41.3 0.1 copy.32
  41.4 0.1 reshape.57.corner_links
  41.5 0.1 copy.33
  41.6 0.1 reshape.58.corner_codes
  41.7 0.0 copy-start.6
  41.7 0.0 copy-start.7
  41.7 0.0 copy-start.8
  41.7 0.2 copy_bitcast_fusion
  41.9 0.5 copy-done.6
  42.4 0.0 copy-done.7
  42.4 0.0 copy-done.8
  42.4 17.1 %shard_map.166 = (bf16[8,192,256]{2,1,0:T(8,128)(2,1)S(1)}, f32[2,1536,128]{2,1,0:T(8,128)}, bf16[96,8,256]{2,1,0:T(8,128)(2,1)S(1)}, bf16[12,8,256]{2,1,0:T(8,1...) custom-call(s32[1]{0:T(128)} %bitcast.me_ref, ...), custom_call_target="tpu_custom_call" | custom-call | tf_op jit(solution)/shard_map/pallas_call | solution.py:509
  60.2 1.3 %copy-done.4 = bf16[2304,256]{1,0:T(8,128)(2,1)S(1)} copy-done((bf16[2304,256]{1,0:T(8,128)(2,1)S(1)}, bf16[2304,256]{1,0:T(8,128)(2,1)}, u32[]{:S(2)}) %copy-start.4) | copy-done | bytes 1179672
  61.4 1.2 %copy-done.5 = bf16[1920,256]{1,0:T(8,128)(2,1)S(1)} copy-done((bf16[1920,256]{1,0:T(8,128)(2,1)S(1)}, bf16[1920,256]{1,0:T(8,128)(2,1)}, u32[]{:S(2)}) %copy-start.5) | copy-done | bytes 983064
  62.6 43.8 %shard_map.167 = (f32[9,32,256]{2,1,0:T(8,128)S(1)}, bf16[8,40,8,256]{3,2,1,0:T(8,128)(2,1)}) custom-call(s32[28]{0:T(128)S(1)} %fusion.index, s32[1]{0:T(128)S(6)} %min.6.bit, bf16[1920,256]{1,0:T(8,128)(2,1)S(1)} %get-tuple-element.20.x0, bf16[1920,256]{1,0:T(8,128)(2,1)S(1)} %get-tuple-element.21.x1, bf16[1920,256]{1,0:T(8,128)(2,1)S(1)} %copy-done.5, ...), custom_call_target="tpu_custom_call" | custom-call | tf_op jit(solution)/shard_map/pallas_call | solution.py:530
  106.4 1.3 %copy-done.2 = bf16[8,40,8,256]{3,2,1,0:T(8,128)(2,1)S(1)} copy-done((bf16[8,40,8,256]{3,2,1,0:T(8,128)(2,1)S(1)}, bf16[8,40,8,256]{3,2,1,0:T(8,128)(2,1)}, u32[]{:S(2)}) %copy-start.2) | copy-done | bytes 1310744
  107.8 3.5 %shard_map.168 = bf16[8,192,256]{2,1,0:T(8,128)(2,1)S(1)} custom-call(s32[1]{0:T(128)} %bitcast.me_ref, s32[96]{0:T(128)S(1)} %reshape.55.links, s32[96]{0:T(128)S(1)} %reshape.56.codes, s32[96]{0:T(128)S(1)} %reshape.57.corner_links, s32[96]{0:T(128)S(1)} %reshape.58.corner_codes, s32[768]{0:T(1024)S(1)} %copy-done.6, f32[2,1536,128]{2,1,0:T(8,128)S(1)} %copy-done.1, ...), custom_call_target="tpu_custom_call" | custom-call | tf_op jit(solution)/shard_map/pallas_call | solution.py:561
  111.2 0.0 copy-start.12
  111.2 1.0 copy_bitcast_fusion.1
  112.2 0.2 copy.43
  112.4 0.1 broadcast_in_dim_reshape.3
  112.5 0.0 copy-start.10
  113.2 0.8 multiply_add_fusion
  113.9 1.0 copy_bitcast_fusion.2
  (16 shorter events, 0.1 us)
Async XLA Ops:
  0.6 41.1 %copy-start = (bf16[1,24,8,8,256]{4,3,2,1,0:T(8,128)(2,1)S(1)}, bf16[1,24,8,8,256]{4,3,2,1,0:T(8,128)(2,1)}, u32[]{:S(2)}) copy-start(bf16[1,24,8,8,256]{4,3,2,1,0:T(8,128)(2,1)} %param.15) | copy-start | bytes 2359300
  3.0 1.0 copy-start.11
  3.2 37.5 %copy-start.13 = (s32[192,4]{0,1:T(4,128)S(1)}, s32[192,4]{0,1:T(4,128)}, u32[]{:S(2)}) copy-start(s32[192,4]{0,1:T(4,128)} %param.19) | copy-start | bytes 9220
  3.3 37.5 %copy-start.14 = (s32[192,4]{0,1:T(4,128)S(1)}, s32[192,4]{0,1:T(4,128)}, u32[]{:S(2)}) copy-start(s32[192,4]{0,1:T(4,128)} %param.18) | copy-start | bytes 9220
  3.3 37.9 %copy-start.15 = (s32[192,4]{0,1:T(4,128)S(1)}, s32[192,4]{0,1:T(4,128)}, u32[]{:S(2)}) copy-start(s32[192,4]{0,1:T(4,128)} %param.21) | copy-start | bytes 9220
  3.3 37.9 %copy-start.16 = (s32[192,4]{0,1:T(4,128)S(1)}, s32[192,4]{0,1:T(4,128)}, u32[]{:S(2)}) copy-start(s32[192,4]{0,1:T(4,128)} %param.20) | copy-start | bytes 9220
  3.3 38.4 %copy-start.9 = (bf16[1,24,8,8,256]{4,3,2,1,0:T(8,128)(2,1)S(1)}, bf16[1,24,8,8,256]{4,3,2,1,0:T(8,128)(2,1)}, u32[]{:S(2)}) copy-start(bf16[1,24,8,8,256]{4,3,2,1,0:T(8,128)(2,1)} %param.14) | copy-start | bytes 2359300
  39.7 1.0 copy-start.3
  41.7 0.7 copy-start.6
  41.7 0.7 copy-start.7
  41.7 0.7 copy-start.8
  60.1 1.3 %copy-start.4 = (bf16[2304,256]{1,0:T(8,128)(2,1)S(1)}, bf16[2304,256]{1,0:T(8,128)(2,1)}, u32[]{:S(2)}) copy-start(bf16[2304,256]{1,0:T(8,128)(2,1)} %get-tuple-element.23.dpre) | copy-start | bytes 3538948
  61.4 1.2 %copy-start.5 = (bf16[1920,256]{1,0:T(8,128)(2,1)S(1)}, bf16[1920,256]{1,0:T(8,128)(2,1)}, u32[]{:S(2)}) copy-start(bf16[1920,256]{1,0:T(8,128)(2,1)} %get-tuple-element.22.x2) | copy-start | bytes 2949124
  62.6 43.8 %copy-start.1 = (f32[2,1536,128]{2,1,0:T(8,128)S(1)}, f32[2,1536,128]{2,1,0:T(8,128)}, u32[]{:S(2)}) copy-start(f32[2,1536,128]{2,1,0:T(8,128)} %get-tuple-element.19.inner) | copy-start | bytes 4718596
  106.4 1.3 %copy-start.2 = (bf16[8,40,8,256]{3,2,1,0:T(8,128)(2,1)S(1)}, bf16[8,40,8,256]{3,2,1,0:T(8,128)(2,1)}, u32[]{:S(2)}) copy-start(bf16[8,40,8,256]{3,2,1,0:T(8,128)(2,1)} %get-tuple-element.26.all_pack) | copy-start | bytes 3932164
  111.2 1.9 %copy-start.12 = (f32[1,288,256]{2,1,0:T(8,128)S(1)}, f32[1,288,256]{2,1,0:T(8,128)}, u32[]{:S(2)}) copy-start(f32[1,288,256]{2,1,0:T(8,128)} %param.17) | copy-start | bytes 884740
  112.5 2.4 %copy-start.10 = (f32[1,288,256]{2,1,0:T(8,128)}, f32[1,288,256]{2,1,0:T(8,128)S(1)}, u32[]{:S(2)}) copy-start(f32[1,288,256]{2,1,0:T(8,128)S(1)} %broadcast_in_dim_reshape.3) | copy-start | bytes 884740
